TPU v7x, 32 devices: a whole 2x2x4 slice. The times are simulated.
32 devices in a mesh: dp: 8 (over y, x, core), tensor: 4 (over z).
Axes of the slice: x: 2, y: 2, z: 4, core: 2. Of those that a mesh axis runs over, the one named last changes fastest.
Arguments:
- pixels: bfloat16 [24576, 768], P('dp'), may hold values from -6 to 6
- coords: int32 [2, 24576], P(None, 'dp'), may hold values from 0 to 63
- lengths: int32 [24, 8], P('dp'), may hold values from 1 to 512, 1024 in all within a row
- labels: int32 [192, 1000], P('dp'), may hold values 0 or 1
- patch_table: float32 [768, 768], P(None, 'dp'), may hold values from -0.21875 to 0.21875
- patch_first: float32 [768, 768], P(None, 'dp'), may hold values from -0.00010681152 to 0.00010681152
- patch_second: float32 [768, 768], P(None, 'dp'), may hold values from 2.928355e-10 to 1.171342e-09
- position_table: float32 [2, 64, 768], P(None, None, 'dp'), may hold values from -3 to 3
- position_first: float32 [2, 64, 768], P(None, None, 'dp'), may hold values from -0.00010681152 to 0.00010681152
- position_second: float32 [2, 64, 768], P(None, None, 'dp'), may hold values from 5.85671e-11 to 2.342684e-10
- attend_in: float32 [768, 3, 768], P('dp', None, 'tensor'), may hold values from -0.21875 to 0.21875
- attend_in_first: float32 [768, 3, 768], P('dp', None, 'tensor'), may hold values from -0.00010681152 to 0.00010681152
- attend_in_second: float32 [768, 3, 768], P('dp', None, 'tensor'), may hold values from 2.928355e-10 to 1.171342e-09
- attend_out: float32 [768, 768], P('tensor', 'dp'), may hold values from -1.75 to 1.75
- attend_out_first: float32 [768, 768], P('tensor', 'dp'), may hold values from -0.00010681152 to 0.00010681152
- attend_out_second: float32 [768, 768], P('tensor', 'dp'), may hold values from 5.85671e-11 to 2.342684e-10
- expand: float32 [768, 3072], P('dp', 'tensor'), may hold values from -0.21875 to 0.21875
- expand_first: float32 [768, 3072], P('dp', 'tensor'), may hold values from -0.00010681152 to 0.00010681152
- expand_second: float32 [768, 3072], P('dp', 'tensor'), may hold values from 2.928355e-10 to 1.171342e-09
- shrink: float32 [3072, 768], P('tensor', 'dp'), may hold values from -0.109375 to 0.109375
- shrink_first: float32 [3072, 768], P('tensor', 'dp'), may hold values from -0.00010681152 to 0.00010681152
- shrink_second: float32 [3072, 768], P('tensor', 'dp'), may hold values from 2.928355e-10 to 1.171342e-09
- classify: float32 [768, 1000], P('dp'), may hold values from -0.875 to 0.875
- classify_first: float32 [768, 1000], P('dp'), may hold values from -0.00010681152 to 0.00010681152
- classify_second: float32 [768, 1000], P('dp'), may hold values from 2.928355e-10 to 1.171342e-09
- vectors: float32 [4, 768], replicated, may hold values from -3 to 3
- vectors_first: float32 [4, 768], replicated, may hold values from -0.0004272461 to 0.0004272461
- vectors_second: float32 [4, 768], replicated, may hold values from 4.685368e-09 to 1.8741472e-08
- head_gains: float32 [2, 64], replicated, may hold values from 0.5 to 1.5
- head_gains_first: float32 [2, 64], replicated, may hold values from -0.0004272461 to 0.0004272461
- head_gains_second: float32 [2, 64], replicated, may hold values from 4.685368e-09 to 1.8741472e-08
Outputs:
- patch_new: float32 [768, 768], P(None, 'dp')
- patch_first_new: float32 [768, 768], P(None, 'dp')
- patch_second_new: float32 [768, 768], P(None, 'dp')
- position_new: float32 [2, 64, 768], P(None, None, 'dp')
- position_first_new: float32 [2, 64, 768], P(None, None, 'dp')
- position_second_new: float32 [2, 64, 768], P(None, None, 'dp')
- attend_in_new: float32 [768, 3, 768], P('dp', None, 'tensor')
- attend_in_first_new: float32 [768, 3, 768], P('dp', None, 'tensor')
- attend_in_second_new: float32 [768, 3, 768], P('dp', None, 'tensor')
- attend_out_new: float32 [768, 768], P('tensor', 'dp')
- attend_out_first_new: float32 [768, 768], P('tensor', 'dp')
- attend_out_second_new: float32 [768, 768], P('tensor', 'dp')
- expand_new: float32 [768, 3072], P('dp', 'tensor')
- expand_first_new: float32 [768, 3072], P('dp', 'tensor')
- expand_second_new: float32 [768, 3072], P('dp', 'tensor')
- shrink_new: float32 [3072, 768], P('tensor', 'dp')
- shrink_first_new: float32 [3072, 768], P('tensor', 'dp')
- shrink_second_new: float32 [3072, 768], P('tensor', 'dp')
- classify_new: float32 [768, 1000], P('dp')
- classify_first_new: float32 [768, 1000], P('dp')
- classify_second_new: float32 [768, 1000], P('dp')
- vectors_new: float32 [4, 768], replicated
- vectors_first_new: float32 [4, 768], replicated
- vectors_second_new: float32 [4, 768], replicated
- head_gains_new: float32 [2, 64], replicated
- head_gains_first_new: float32 [2, 64], replicated
- head_gains_second_new: float32 [2, 64], replicated
- loss_value: float32 [], replicated
- grad_norm: float32 [], replicated
Inputs may be any that keep to these rules, and one draw needn't show every extreme that they name: Each pack's 8 image lengths add up to 1024.
All inputs are finite; a program needn't handle non-finite values. No bound on the sum of `labels` on one device may be relied on, other than what follows from the above.
Results may differ from a plain program's by a relative error of at most 0.025.
Values may be sent and summed in bfloat16 or wider, within the bound.
A program may use at most 256 MiB of HBM per device.

v0:
```python
import jax
import jax.numpy as jnp
from jax import lax
from jax.sharding import PartitionSpec as P

STEP = 10


NEGATIVE = -1e30
NORM_EPS = 1e-06
CLIP = 0.05
RATE_BASE = 0.03
RATE_POSITION = 0.2
RATE_MIDDLE = 0.1
RATE_VECTOR = 1.0
DECAY = 0.05
BETA_ONE = 0.5
BETA_TWO = 0.5
ADAM_EPS = 1e-08
SHIFT = -4.0
HIGH = lax.Precision.HIGHEST


def layer_norm(values, gain_row):
    center = values - jnp.mean(values, axis=-1, keepdims=True)
    inverse = lax.rsqrt(jnp.mean(center * center, axis=-1, keepdims=True) + NORM_EPS)
    normed = center * inverse
    return (normed * gain_row, normed, inverse)


def norm_back(gradient, gain_row, normed, inverse):
    scaled = gradient * gain_row
    d_input = inverse * (
        scaled
        - jnp.mean(scaled, axis=-1, keepdims=True)
        - normed * jnp.mean(scaled * normed, axis=-1, keepdims=True)
    )
    gain_grad = jnp.sum((gradient * normed).reshape(-1, gain_row.shape[-1]), axis=0)
    return (d_input, gain_grad)


def image_index(lengths, pack_rows):
    image_ends = jnp.cumsum(lengths, axis=-1)
    positions = lax.broadcasted_iota(jnp.int32, (lengths.shape[0], pack_rows, 1), 1)
    image_ids = jnp.sum((positions >= image_ends[:, None, :]).astype(jnp.int32), axis=-1)
    slots = lax.broadcasted_iota(jnp.int32, (1, 1, lengths.shape[1]), 2)
    return (image_ids, image_ids[:, :, None] == slots)


def block_scores(query_part, key_rows, part_ids, image_ids):
    scaling = query_part.shape[-1] ** (-0.5)
    scores = (
        jnp.einsum("qhd,khd->hqk", query_part, key_rows, preferred_element_type=jnp.float32)
        * scaling
    )
    return jnp.where((part_ids[:, None] == image_ids[None, :])[None], scores, NEGATIVE)


def attend_pack(query_rows, key_rows, value_rows, image_ids):
    pack_rows = query_rows.shape[0]
    block_rows = min(512, pack_rows)

    def forward_block(block_index):
        start = block_index * block_rows
        query_part = lax.dynamic_slice_in_dim(query_rows, start, block_rows, 0)
        part_ids = lax.dynamic_slice_in_dim(image_ids, start, block_rows, 0)
        scores = block_scores(query_part, key_rows, part_ids, image_ids)
        row_peak = jnp.max(scores, axis=-1, keepdims=True)
        exponent = jnp.exp(scores - row_peak)
        row_total = jnp.sum(exponent, axis=-1, keepdims=True)
        probability = (exponent / row_total).astype(jnp.bfloat16)
        attended_block = jnp.einsum(
            "hqk,khd->qhd", probability, value_rows, preferred_element_type=jnp.float32
        )
        return (attended_block.astype(jnp.bfloat16), (row_peak + jnp.log(row_total))[..., 0])

    attended, log_totals = lax.map(forward_block, jnp.arange(pack_rows // block_rows))
    heads_here = query_rows.shape[1]
    return (
        attended.reshape(pack_rows, heads_here, query_rows.shape[2]),
        jnp.transpose(log_totals, (1, 0, 2)).reshape(heads_here, pack_rows),
    )


def attend_back(query_rows, key_rows, value_rows, image_ids, log_totals, grad_rows):
    pack_rows = query_rows.shape[0]
    block_rows = min(512, pack_rows)
    scaling = query_rows.shape[-1] ** (-0.5)

    def backward_block(running, block_index):
        d_keys, d_values = running
        start = block_index * block_rows
        query_part = lax.dynamic_slice_in_dim(query_rows, start, block_rows, 0)
        part_ids = lax.dynamic_slice_in_dim(image_ids, start, block_rows, 0)
        part_totals = lax.dynamic_slice_in_dim(log_totals, start, block_rows, 1)
        part_grad = lax.dynamic_slice_in_dim(grad_rows, start, block_rows, 0)
        scores = block_scores(query_part, key_rows, part_ids, image_ids)
        probability = jnp.exp(scores - part_totals[..., None])
        d_probs = jnp.einsum(
            "qhd,khd->hqk", part_grad, value_rows, preferred_element_type=jnp.float32
        )
        d_scores = (
            probability
            * (d_probs - jnp.sum(probability * d_probs, axis=-1, keepdims=True))
            * scaling
        ).astype(jnp.bfloat16)
        d_query = jnp.einsum("hqk,khd->qhd", d_scores, key_rows, preferred_element_type=jnp.float32)
        d_keys = d_keys + jnp.einsum(
            "hqk,qhd->khd", d_scores, query_part, preferred_element_type=jnp.float32
        )
        d_values = d_values + jnp.einsum(
            "hqk,qhd->khd",
            probability.astype(jnp.bfloat16),
            part_grad,
            preferred_element_type=jnp.float32,
        )
        return ((d_keys, d_values), d_query)

    blank = jnp.zeros(key_rows.shape, jnp.float32)
    (d_keys, d_values), d_query = lax.scan(
        backward_block, (blank, blank), jnp.arange(pack_rows // block_rows)
    )
    return (d_query.reshape(query_rows.shape), d_keys, d_values)


def adam(master, first_moment, second_moment, gradient, clip_scale, rate, decay_rate):
    gradient = gradient * clip_scale
    first_new = BETA_ONE * first_moment + (1 - BETA_ONE) * gradient
    second_new = BETA_TWO * second_moment + (1 - BETA_TWO) * gradient * gradient
    update = (
        first_new / (1 - BETA_ONE**STEP) / (jnp.sqrt(second_new / (1 - BETA_TWO**STEP)) + ADAM_EPS)
    )
    return (master - rate * (update + decay_rate * master), first_new, second_new)


def squared(entry):
    return jnp.sum(entry * entry)


def per_device(
    pixels,
    coords,
    lengths,
    labels,
    patch_table,
    patch_first,
    patch_second,
    position_table,
    position_first,
    position_second,
    attend_in,
    attend_in_first,
    attend_in_second,
    attend_out,
    attend_out_first,
    attend_out_second,
    expand,
    expand_first,
    expand_second,
    shrink,
    shrink_first,
    shrink_second,
    classify,
    classify_first,
    classify_second,
    vectors,
    vectors_first,
    vectors_second,
    head_gains,
    head_gains_first,
    head_gains_second,
):
    low_type = jnp.bfloat16
    w_patch, w_pos, w_in, w_out, w_up, w_down, w_head = (
        lax.all_gather(patch_table.astype(low_type), "dp", axis=1, tiled=True),
        lax.all_gather(position_table.astype(low_type), "dp", axis=2, tiled=True),
        lax.all_gather(attend_in.astype(low_type), "dp", axis=0, tiled=True),
        lax.all_gather(attend_out.astype(low_type), "dp", axis=1, tiled=True),
        lax.all_gather(expand.astype(low_type), "dp", axis=0, tiled=True),
        lax.all_gather(shrink.astype(low_type), "dp", axis=1, tiled=True),
        lax.all_gather(classify.astype(low_type), "dp", axis=0, tiled=True),
    )
    pack_count = lengths.shape[0]
    tokens = pixels.shape[0]
    pack_rows = tokens // pack_count
    model_width = w_patch.shape[1]
    head_size = head_gains.shape[1]
    local_heads = w_in.shape[2] // head_size
    position_grid = lax.broadcasted_iota(jnp.int32, (1, w_pos.shape[1]), 1)
    one_x = (coords[0][:, None] == position_grid).astype(low_type)
    one_y = (coords[1][:, None] == position_grid).astype(low_type)
    embedded = (
        jnp.dot(pixels, w_patch, preferred_element_type=jnp.float32)
        + jnp.dot(one_x, w_pos[0], preferred_element_type=jnp.float32)
        + jnp.dot(one_y, w_pos[1], preferred_element_type=jnp.float32)
    )
    first_norm, normed_one, inverse_one = layer_norm(embedded, vectors[0])
    first_low = first_norm.astype(low_type)
    joined = jnp.einsum("td,dcf->tcf", first_low, w_in, preferred_element_type=jnp.float32).reshape(
        tokens, 3, local_heads, head_size
    )
    query_norm, query_normed, query_inverse = layer_norm(joined[:, 0], head_gains[0])
    key_norm, key_normed, key_inverse = layer_norm(joined[:, 1], head_gains[1])
    stacked_shape = (pack_count, pack_rows, local_heads, head_size)
    query_low = query_norm.astype(low_type).reshape(stacked_shape)
    key_low = key_norm.astype(low_type).reshape(stacked_shape)
    value_low = joined[:, 2].astype(low_type).reshape(stacked_shape)
    image_ids, members = image_index(lengths, pack_rows)
    attended, log_totals = lax.map(
        lambda pack_item: attend_pack(*pack_item), (query_low, key_low, value_low, image_ids)
    )
    attended = attended.reshape(tokens, local_heads * head_size)
    middle = embedded + lax.psum(
        jnp.dot(attended, w_out, preferred_element_type=jnp.float32).astype(jnp.bfloat16), "tensor"
    ).astype(jnp.float32)
    second_norm, normed_two, inverse_two = layer_norm(middle, vectors[1])
    second_low = second_norm.astype(low_type)
    hidden = jnp.dot(second_low, w_up, preferred_element_type=jnp.float32)
    active_low = jax.nn.gelu(hidden, approximate=False).astype(low_type)
    output_rows = middle + lax.psum(
        jnp.dot(active_low, w_down, preferred_element_type=jnp.float32).astype(jnp.bfloat16),
        "tensor",
    ).astype(jnp.float32)
    last_norm, normed_three, inverse_three = layer_norm(output_rows, vectors[2])
    root_width = model_width**0.5
    last_packed = last_norm.reshape(pack_count, pack_rows, model_width)
    pool_logit = jnp.sum(last_packed * vectors[3], axis=-1) / root_width
    masked = jnp.where(members, pool_logit[:, :, None], NEGATIVE)
    exponent = jnp.exp(masked - jnp.max(masked, axis=1, keepdims=True))
    pool_weights = exponent / jnp.sum(exponent, axis=1, keepdims=True)
    pooled = jnp.einsum("psi,psd->pid", pool_weights, last_packed, precision=HIGH)
    images = pack_count * lengths.shape[1]
    pooled_low = pooled.reshape(images, model_width).astype(low_type)
    logits = jnp.dot(pooled_low, w_head, preferred_element_type=jnp.float32) + SHIFT
    targets = labels.astype(jnp.float32)
    loss_local = jnp.sum(jax.nn.softplus(logits) - targets * logits)
    image_count = images * lax.axis_size("dp")
    d_logits = ((jax.nn.sigmoid(logits) - targets) / image_count).astype(low_type)
    grad_head = jnp.dot(pooled_low.T, d_logits, preferred_element_type=jnp.float32)
    d_pooled = jnp.dot(d_logits, w_head.T, preferred_element_type=jnp.float32).reshape(
        pack_count, lengths.shape[1], model_width
    )
    d_weights = jnp.einsum("pid,psd->psi", d_pooled, last_packed, precision=HIGH)
    d_masked = pool_weights * (d_weights - jnp.sum(pool_weights * d_weights, axis=1, keepdims=True))
    d_pool_logit = jnp.sum(d_masked, axis=-1)
    d_last = (
        jnp.einsum("psi,pid->psd", pool_weights, d_pooled, precision=HIGH)
        + d_pool_logit[..., None] * vectors[3] / root_width
    )
    grad_query_vector = jnp.sum(d_pool_logit[..., None] * last_packed, axis=(0, 1)) / root_width
    d_output, grad_gain_three = norm_back(
        d_last.reshape(tokens, model_width), vectors[2], normed_three, inverse_three
    )
    branch_grad = d_output.astype(low_type)
    grad_down = jnp.dot(active_low.T, branch_grad, preferred_element_type=jnp.float32)
    d_active = jnp.dot(branch_grad, w_down.T, preferred_element_type=jnp.float32)
    d_hidden = jax.vjp(lambda inner: jax.nn.gelu(inner, approximate=False), hidden)[1](d_active)[
        0
    ].astype(low_type)
    grad_up = jnp.dot(second_low.T, d_hidden, preferred_element_type=jnp.float32)
    d_second = lax.psum(
        jnp.dot(d_hidden, w_up.T, preferred_element_type=jnp.float32).astype(jnp.bfloat16), "tensor"
    ).astype(jnp.float32)
    d_middle_part, grad_gain_two = norm_back(d_second, vectors[1], normed_two, inverse_two)
    d_middle = d_output + d_middle_part
    attend_grad = d_middle.astype(low_type)
    grad_out = jnp.dot(attended.T, attend_grad, preferred_element_type=jnp.float32)
    d_attended = (
        jnp.dot(attend_grad, w_out.T, preferred_element_type=jnp.float32)
        .astype(low_type)
        .reshape(stacked_shape)
    )
    d_query, d_key, d_value = lax.map(
        lambda pack_item: attend_back(*pack_item),
        (query_low, key_low, value_low, image_ids, log_totals, d_attended),
    )
    head_shape = (tokens, local_heads, head_size)
    d_query_raw, grad_query_gain = norm_back(
        d_query.reshape(head_shape), head_gains[0], query_normed, query_inverse
    )
    d_key_raw, grad_key_gain = norm_back(
        d_key.reshape(head_shape), head_gains[1], key_normed, key_inverse
    )
    d_joined = (
        jnp.stack([d_query_raw, d_key_raw, d_value.reshape(head_shape)], axis=1)
        .reshape(tokens, 3, local_heads * head_size)
        .astype(low_type)
    )
    grad_in = jnp.einsum("td,tcf->dcf", first_low, d_joined, preferred_element_type=jnp.float32)
    d_first = lax.psum(
        jnp.einsum("tcf,dcf->td", d_joined, w_in, preferred_element_type=jnp.float32).astype(
            jnp.bfloat16
        ),
        "tensor",
    ).astype(jnp.float32)
    d_embed_part, grad_gain_one = norm_back(d_first, vectors[0], normed_one, inverse_one)
    embed_grad = (d_middle + d_embed_part).astype(low_type)
    grad_patch = jnp.dot(pixels.T, embed_grad, preferred_element_type=jnp.float32)
    grad_pos = jnp.stack(
        [
            jnp.dot(one_x.T, embed_grad, preferred_element_type=jnp.float32),
            jnp.dot(one_y.T, embed_grad, preferred_element_type=jnp.float32),
        ]
    )
    leader = (lax.axis_index("tensor") == 0).astype(jnp.float32)
    grad_vectors = (
        jnp.stack([grad_gain_one, grad_gain_two, grad_gain_three, grad_query_vector]) * leader
    )
    grad_gains = jnp.stack([grad_query_gain, grad_key_gain])
    grad_vectors, grad_gains, loss_total = lax.psum(
        (grad_vectors, grad_gains, loss_local * leader), ("dp", "tensor")
    )
    share_patch, share_pos, share_in, share_out, share_up, share_down, share_head = (
        lax.psum_scatter(grad_patch, "dp", scatter_dimension=1, tiled=True),
        lax.psum_scatter(grad_pos, "dp", scatter_dimension=2, tiled=True),
        lax.psum_scatter(grad_in, "dp", scatter_dimension=0, tiled=True),
        lax.psum_scatter(grad_out, "dp", scatter_dimension=1, tiled=True),
        lax.psum_scatter(grad_up, "dp", scatter_dimension=0, tiled=True),
        lax.psum_scatter(grad_down, "dp", scatter_dimension=1, tiled=True),
        lax.psum_scatter(grad_head, "dp", scatter_dimension=0, tiled=True),
    )
    split_squares = squared(share_in) + squared(share_out) + squared(share_up) + squared(share_down)
    whole_squares = squared(share_patch) + squared(share_pos) + squared(share_head)
    squares = lax.psum(split_squares + leader * whole_squares, ("dp", "tensor"))
    grad_norm = jnp.sqrt(squares + squared(grad_vectors) + squared(grad_gains))
    clip_scale = CLIP / jnp.maximum(grad_norm, CLIP)
    patch_new = adam(
        patch_table, patch_first, patch_second, share_patch, clip_scale, RATE_BASE, DECAY
    )
    position_new = adam(
        position_table, position_first, position_second, share_pos, clip_scale, RATE_POSITION, DECAY
    )
    attend_in_new = adam(
        attend_in, attend_in_first, attend_in_second, share_in, clip_scale, RATE_BASE, DECAY
    )
    attend_out_new = adam(
        attend_out, attend_out_first, attend_out_second, share_out, clip_scale, RATE_MIDDLE, DECAY
    )
    expand_new = adam(expand, expand_first, expand_second, share_up, clip_scale, RATE_BASE, DECAY)
    shrink_new = adam(shrink, shrink_first, shrink_second, share_down, clip_scale, RATE_BASE, DECAY)
    classify_new = adam(
        classify, classify_first, classify_second, share_head, clip_scale, RATE_MIDDLE, DECAY
    )
    vectors_new = adam(
        vectors, vectors_first, vectors_second, grad_vectors, clip_scale, RATE_VECTOR, 0.0
    )
    gains_new = adam(
        head_gains, head_gains_first, head_gains_second, grad_gains, clip_scale, RATE_VECTOR, 0.0
    )
    return (
        patch_new[0],
        patch_new[1],
        patch_new[2],
        position_new[0],
        position_new[1],
        position_new[2],
        attend_in_new[0],
        attend_in_new[1],
        attend_in_new[2],
        attend_out_new[0],
        attend_out_new[1],
        attend_out_new[2],
        expand_new[0],
        expand_new[1],
        expand_new[2],
        shrink_new[0],
        shrink_new[1],
        shrink_new[2],
        classify_new[0],
        classify_new[1],
        classify_new[2],
        vectors_new[0],
        vectors_new[1],
        vectors_new[2],
        gains_new[0],
        gains_new[1],
        gains_new[2],
        loss_total,
        grad_norm,
    )


def solution(mesh):
    in_specs = (
        P("dp", None),
        P(None, "dp"),
        P("dp", None),
        P("dp", None),
        P(None, "dp"),
        P(None, "dp"),
        P(None, "dp"),
        P(None, None, "dp"),
        P(None, None, "dp"),
        P(None, None, "dp"),
        P("dp", None, "tensor"),
        P("dp", None, "tensor"),
        P("dp", None, "tensor"),
        P("tensor", "dp"),
        P("tensor", "dp"),
        P("tensor", "dp"),
        P("dp", "tensor"),
        P("dp", "tensor"),
        P("dp", "tensor"),
        P("tensor", "dp"),
        P("tensor", "dp"),
        P("tensor", "dp"),
        P("dp", None),
        P("dp", None),
        P("dp", None),
        P(),
        P(),
        P(),
        P(),
        P(),
        P(),
    )
    out_specs = (
        P(None, "dp"),
        P(None, "dp"),
        P(None, "dp"),
        P(None, None, "dp"),
        P(None, None, "dp"),
        P(None, None, "dp"),
        P("dp", None, "tensor"),
        P("dp", None, "tensor"),
        P("dp", None, "tensor"),
        P("tensor", "dp"),
        P("tensor", "dp"),
        P("tensor", "dp"),
        P("dp", "tensor"),
        P("dp", "tensor"),
        P("dp", "tensor"),
        P("tensor", "dp"),
        P("tensor", "dp"),
        P("tensor", "dp"),
        P("dp", None),
        P("dp", None),
        P("dp", None),
        P(),
        P(),
        P(),
        P(),
        P(),
        P(),
        P(),
        P(),
    )
    return jax.shard_map(
        per_device, mesh=mesh, in_specs=in_specs, out_specs=out_specs, check_vma=False
    )
```

profile of v0, /device:TPU:0, one launch (start us, length us, event | category | flops | bytes accessed | tf_op | source)
XLA Modules:
  0.0 1799.7 jit_solution(2261743230477932101)
XLA Ops:
  10.0 11.0 all_gather.22
  23.3 16.6 all_gather.23
  41.1 9.6 all_gather.24
  57.0 10.3 fusion.179
  110.8 63.0 %while.54 = (s32[]{:T(128)}, bf16[3,1024,3,64]{3,2,1,0:T(4,128)(2,1)}, f32[3,3,1024]{2,1,0:T(4,128)}, bf16[3,1024,3,64]{1,3,2,0:T(8,128)(2,1)S(1)}, s32[3,1024]{...) while((s32[]{:T(128)}, ...), condition=%wide.region_13.14_spmd, body=%wide.region_8.13_spmd.sunk | while | flops 422148608 | bytes 28415952 | solution.py:209
  112.7 15.5 while.57
  133.7 15.5 while.57
  154.7 15.5 while.57
  187.8 170.6 %all-reduce.6.cloned.1.call-done = bf16[3072,768]{1,0:T(8,128)(2,1)} async-done(((bf16[3072,768]{1,0:T(8,128)(2,1)}), bf16[3072,768]{1,0:T(8,128)(2,1)}) %all-reduce.6.cloned.1.call-update) | async-done | bytes 4718608 | tf_op jit(solution)/shard_map/psum | solution.py:213
  358.4 9.7 fusion.174
  384.0 26.4 %multiply_convert_fusion.1 = (bf16[3072,768]{1,0:T(8,128)(2,1)}, f32[3072,768]{1,0:T(8,128)}, f32[3072,768]{1,0:T(8,128)}) fusion(bf16[3072,768]{1,0:T(8,128)(2,1)} %multiply_convert_fusion.2, bf16[768,768]{1,0:T(8,128)(2,1)} %all-gather.7.cloned.1.call-done), kind=kOutput, calls=%fused_computation.111 | convolution fusion | flops 3777232896 | bytes 29491200 | tf_op jit(solution)/shard_map/dot_general | solution.py:218
  420.4 170.9 %all-reduce.8.cloned.1.call-done = bf16[3072,768]{1,0:T(8,128)(2,1)} async-done(((bf16[3072,768]{1,0:T(8,128)(2,1)}), bf16[3072,768]{1,0:T(8,128)(2,1)}) %all-reduce.8.cloned.1.call-update) | async-done | bytes 4718608 | tf_op jit(solution)/shard_map/psum | solution.py:220
  591.3 9.6 fusion.172
  624.1 10.8 fusion.181
  635.1 9.6 multiply_reduce_fusion.3
  657.1 15.5 add_convert_fusion
  680.7 171.3 %all-reduce.10.cloned.1.call-done = bf16[3072,768]{1,0:T(8,128)(2,1)} async-done(((bf16[3072,768]{1,0:T(8,128)(2,1)}), bf16[3072,768]{1,0:T(8,128)(2,1)}) %all-reduce.10.cloned.1.call-update) | async-done | bytes 4718608 | tf_op jit(solution)/shard_map/psum | solution.py:261
  852.0 9.1 fusion.92
  876.6 322.8 %while.56 = (s32[]{:T(128)}, f32[3,1024,3,64]{3,2,1,0:T(4,128)}, f32[3,1024,3,64]{1,0,3,2:T(4,128)}, bf16[3,1024,3,64]{1,3,2,0:T(8,128)(2,1)}, bf16[3,1024,3,64]...) while((s32[]{:T(128)}, f32[3,1024,3,64]{3,2,1,0:T(4,128)}, ...), condition=%wide.region_34.35_spmd, body=%wide.region_30.34_spmd.sunk | while | flops 1048843264 | bytes 90275864 | solution.py:273
  880.1 82.8 %while.58 = (s32[]{:T(128)}, f32[1024,3,64]{0,2,1:T(8,128)S(1)}, f32[1024,3,64]{0,2,1:T(8,128)}, f32[2,512,3,64]{1,3,2,0:T(8,128)}, s32[2]{0:T(128)S(1)}, /*inde...) while((s32[]{:T(128)}, f32[1024,3,64]{0,2,1:T(8,128)S(1)}, ...), condition=%wide.region_33.33_spmd.clone, body=%wide.region_31.32_spmd.clone.sunk | while | flops 1048843264 | bytes 77921000 | solution.py:120
  889.0 13.4 fusion.256
  902.4 13.6 fusion.254
  930.3 13.4 fusion.256
  943.7 13.5 fusion.254
  967.2 15.3 dynamic_update_slice.50
  987.5 82.9 %while.58 = (s32[]{:T(128)}, f32[1024,3,64]{0,2,1:T(8,128)S(1)}, f32[1024,3,64]{0,2,1:T(8,128)}, f32[2,512,3,64]{1,3,2,0:T(8,128)}, s32[2]{0:T(128)S(1)}, /*inde...) while((s32[]{:T(128)}, f32[1024,3,64]{0,2,1:T(8,128)S(1)}, ...), condition=%wide.region_33.33_spmd.clone, body=%wide.region_31.32_spmd.clone.sunk | while | flops 1048843264 | bytes 77921000 | solution.py:120
  996.4 13.4 fusion.256
  1009.8 13.6 fusion.254
  1037.8 13.4 fusion.256
  1051.1 13.6 fusion.254
  1074.7 15.3 dynamic_update_slice.50
  1095.0 82.9 %while.58 = (s32[]{:T(128)}, f32[1024,3,64]{0,2,1:T(8,128)S(1)}, f32[1024,3,64]{0,2,1:T(8,128)}, f32[2,512,3,64]{1,3,2,0:T(8,128)}, s32[2]{0:T(128)S(1)}, /*inde...) while((s32[]{:T(128)}, f32[1024,3,64]{0,2,1:T(8,128)S(1)}, ...), condition=%wide.region_33.33_spmd.clone, body=%wide.region_31.32_spmd.clone.sunk | while | flops 1048843264 | bytes 77921000 | solution.py:120
  1103.9 13.4 fusion.256
  1117.3 13.6 fusion.254
  1145.2 13.4 fusion.256
  1158.6 13.6 fusion.254
  1182.2 15.3 dynamic_update_slice.50
  1250.1 11.3 fusion.116
  1261.4 9.0 fusion.182
  1288.5 132.5 %all-reduce.12.cloned.1.call-done = bf16[3072,768]{1,0:T(8,128)(2,1)} async-done(((bf16[3072,768]{1,0:T(8,128)(2,1)}), bf16[3072,768]{1,0:T(8,128)(2,1)}) %all-reduce.12.cloned.1.call-update) | async-done | bytes 4718608 | tf_op jit(solution)/shard_map/psum | solution.py:290
  1443.2 9.5 convolution_bitcast_fusion
  1467.5 44.4 %reduce-scatter.16.cloned.1.call-done = f32[96,768]{1,0:T(8,128)} async-done(((f32[768,768]{1,0:T(8,128)}), f32[96,768]{1,0:T(8,128)}) %reduce-scatter.16.cloned.1.call-update) | async-done | bytes 294928 | tf_op jit(solution)/shard_map/reduce_scatter | solution.py:318
  1513.6 47.9 %reduce-scatter.20.cloned.1.call-done = f32[96,1000]{1,0:T(8,128)} async-done(((f32[768,1000]{1,0:T(8,128)}), f32[96,1000]{1,0:T(8,128)}) %reduce-scatter.20.cloned.1.call-update) | async-done | bytes 384016 | tf_op jit(solution)/shard_map/reduce_scatter | solution.py:320
  1563.3 36.6 %reduce-scatter.22.cloned.1.call-done = f32[96,192]{1,0:T(8,128)} async-done(((f32[768,192]{1,0:T(8,128)}), f32[96,192]{1,0:T(8,128)}) %reduce-scatter.22.cloned.1.call-update) | async-done | bytes 73744
  1601.5 44.6 %reduce-scatter.14.cloned.1.call-done = f32[96,3,192]{2,0,1:T(8,128)} async-done(((f32[768,3,192]{2,0,1:T(8,128)}), f32[96,3,192]{2,0,1:T(8,128)}) %reduce-scatter.14.cloned.1.call-update) | async-done | bytes 221200 | tf_op jit(solution)/shard_map/reduce_scatter | solution.py:316
  1650.4 33.0 %reduce-scatter.24.cloned.1.call-done = f32[96,128]{1,0:T(8,128)} async-done(((f32[768,128]{1,0:T(8,128)}), f32[96,128]{1,0:T(8,128)}) %reduce-scatter.24.cloned.1.call-update) | async-done | bytes 49168
  1685.0 44.1 %reduce-scatter.12.cloned.1.call-done = f32[768,96]{0,1:T(8,128)} async-done(((f32[768,768]{0,1:T(8,128)}), f32[768,96]{0,1:T(8,128)}) %reduce-scatter.12.cloned.1.call-update) | async-done | bytes 294928 | tf_op jit(solution)/shard_map/reduce_scatter | solution.py:314
  1732.8 39.6 %all-reduce = (f32[]{:T(128)}, f32[4,768]{1,0:T(4,128)}, f32[2,64]{1,0:T(2,128)}, f32[]{:T(128)}) all-reduce(f32[]{:T(128)S(6)} %add.324, f32[4,768]{1,0:T(4,128)S(1)} %maximum_multiply_fusion, f32[2,64]{1,0:T(2,128)S(1)} %pad_maximum_fusion.4, f32[]{:T(128)S(6)} %mul.876), channel_id=1, replica_groups=mesh['dp'=8,'tensor'=4] {'dp','tensor'}, use_global_device_ids=true, to_apply=%region_56.57 | all-reduce | flops 3202 | bytes 25616 | tf_op jit(solution)/shard_map/psum | solution.py:324
  (537 shorter events, 456.0 us)
Async XLA Ops:
  7.2 33.6 %copy-start.96 = (s32[3,8]{1,0:T(4,128)S(1)}, s32[3,8]{1,0:T(4,128)}, u32[]{:S(2)}) copy-start(s32[3,8]{1,0:T(4,128)} %param.41) | copy-start | bytes 292
  7.2 33.8 %copy-start.53 = (f32[192,96]{1,0:T(8,128)S(1)}, f32[192,96]{1,0:T(8,128)}, u32[]{:S(2)}) copy-start(f32[192,96]{1,0:T(8,128)} %param.52) | copy-start | bytes 221188
  7.2 43.6 %copy-start.84 = (f32[4,768]{1,0:T(4,128)S(1)}, f32[4,768]{1,0:T(4,128)}, u32[]{:S(2)}) copy-start(f32[4,768]{1,0:T(4,128)} %param.64) | copy-start | bytes 36868
  7.2 44.2 %copy-start.95 = (f32[2,64]{1,0:T(2,128)S(1)}, f32[2,64]{1,0:T(2,128)}, u32[]{:S(2)}) copy-start(f32[2,64]{1,0:T(2,128)} %param.67) | copy-start | bytes 1540
  7.2 44.2 %copy-start.85 = (s32[2,3072]{1,0:T(2,128)S(1)}, s32[2,3072]{1,0:T(2,128)}, u32[]{:S(2)}) copy-start(s32[2,3072]{1,0:T(2,128)} %param.40) | copy-start | bytes 73732
  7.3 49.7 %all-gather.5.cloned.1.call-start = ((), (), s32[]{:S(2)}) async-start(), calls=%async_computation.7 | async-start | bytes 1327104 | tf_op jit(solution)/shard_map/all_gather | solution.py:175
  9.0 349.4 %all-reduce.6.cloned.1.call-start = ((), (), s32[]{:S(2)}) async-start(), calls=%async_computation.8 | async-start | bytes 9437184 | tf_op jit(solution)/shard_map/psum | solution.py:213
  40.8 35.9 %copy-start.37 = (bf16[768,3,192]{0,2,1:T(8,128)(2,1)}, bf16[768,3,192]{0,2,1:T(8,128)(2,1)S(1)}, u32[]{:S(2)}) copy-start(bf16[768,3,192]{0,2,1:T(8,128)(2,1)S(1)} %copy.205) | copy-start | bytes 2654212
  51.5 23.4 %copy-start.80 = (f32[768]{0:T(1024)}, f32[768]{0:T(1024)S(1)}, u32[]{:S(2)}) copy-start(f32[768]{0:T(1024)S(1)} %get-tuple-element.403) | copy-start | bytes 9220
  51.5 43.8 %copy-start.91 = (f32[64]{0:T(128)}, f32[64]{0:T(128)S(1)}, u32[]{:S(2)}) copy-start(f32[64]{0:T(128)S(1)} %get-tuple-element.534) | copy-start | bytes 772
  51.5 51.2 %copy-start.93 = (f32[64]{0:T(128)}, f32[64]{0:T(128)S(1)}, u32[]{:S(2)}) copy-start(f32[64]{0:T(128)S(1)} %get-tuple-element.535) | copy-start | bytes 772
  186.0 197.9 %all-gather.7.cloned.1.call-start = ((), (), s32[]{:S(2)}) async-start(), calls=%async_computation.9 | async-start | bytes 1327104 | tf_op jit(solution)/shard_map/all_gather | solution.py:179
  186.8 223.6 %all-gather.9.cloned.1.call-start = ((), (), s32[]{:S(2)}) async-start(), calls=%async_computation.10 | async-start | bytes 1327104 | tf_op jit(solution)/shard_map/all_gather | solution.py:180
  187.5 403.7 %all-reduce.8.cloned.1.call-start = ((), (), s32[]{:S(2)}) async-start(), calls=%async_computation.11 | async-start | bytes 9437184 | tf_op jit(solution)/shard_map/psum | solution.py:220
  419.2 200.0 %all-gather.11.cloned.1.call-start = ((), (), s32[]{:S(2)}) async-start(), calls=%async_computation.12 | async-start | bytes 1769472 | tf_op jit(solution)/shard_map/all_gather | solution.py:181
  419.9 432.0 %all-reduce.10.cloned.1.call-start = ((), (), s32[]{:S(2)}) async-start(), calls=%async_computation.13 | async-start | bytes 9437184 | tf_op jit(solution)/shard_map/psum | solution.py:261
  672.6 179.3 %copy-start.59 = (f32[3072]{0:T(1024)S(1)}, f32[3072]{0:T(1024)}, u32[]{:S(2)}) copy-start(f32[3072]{0:T(1024)} %copy-done.58) | copy-start | bytes 36868
  672.6 179.3 %copy-start.70 = (f32[3072]{0:T(1024)S(1)}, f32[3072]{0:T(1024)}, u32[]{:S(2)}) copy-start(f32[3072]{0:T(1024)} %copy-done.69) | copy-start | bytes 36868
  672.6 179.3 %copy-start.83 = (f32[768]{0:T(1024)S(1)}, f32[768]{0:T(1024)}, u32[]{:S(2)}) copy-start(f32[768]{0:T(1024)} %get-tuple-element.402) | copy-start | bytes 9220
  680.6 740.3 %all-reduce.12.cloned.1.call-start = ((), (), s32[]{:S(2)}) async-start(), calls=%async_computation.14 | async-start | bytes 9437184 | tf_op jit(solution)/shard_map/psum | solution.py:290
  876.6 322.8 %copy-start.44 = (f32[3,1024,3]{1,0,2:T(4,128)S(1)}, f32[3,1024,3]{1,0,2:T(4,128)}, u32[]{:S(2)}) copy-start(f32[3,1024,3]{1,0,2:T(4,128)} %copy-done.43) | copy-start | bytes 110596
  876.6 322.8 %copy-start.48 = (f32[3,1024,3]{1,0,2:T(4,128)S(1)}, f32[3,1024,3]{1,0,2:T(4,128)}, u32[]{:S(2)}) copy-start(f32[3,1024,3]{1,0,2:T(4,128)} %copy-done.47) | copy-start | bytes 110596
  876.6 322.8 %copy-start.92 = (f32[64]{0:T(128)S(1)}, f32[64]{0:T(128)}, u32[]{:S(2)}) copy-start(f32[64]{0:T(128)} %copy-done.91) | copy-start | bytes 772
  1249.8 216.0 %reduce-scatter.18.cloned.1.call-start = ((), (), s32[]{:S(2)}) async-start(), calls=%async_computation.18 | async-start | bytes 2654208 | tf_op jit(solution)/shard_map/reduce_scatter | solution.py:319
  1261.4 250.5 %reduce-scatter.16.cloned.1.call-start = ((), (), s32[]{:S(2)}) async-start(), calls=%async_computation.17 | async-start | bytes 2654208 | tf_op jit(solution)/shard_map/reduce_scatter | solution.py:318
  1270.5 291.0 %reduce-scatter.20.cloned.1.call-start = ((), (), s32[]{:S(2)}) async-start(), calls=%async_computation.19 | async-start | bytes 3538944 | tf_op jit(solution)/shard_map/reduce_scatter | solution.py:320
  1273.0 326.9 %reduce-scatter.22.cloned.1.call-start = ((), (), s32[]{:S(2)}) async-start(), calls=%async_computation.20 | async-start | bytes 884736
  1279.6 141.3 %copy-start.61 = (f32[3072]{0:T(1024)S(1)}, f32[3072]{0:T(1024)}, u32[]{:S(2)}) copy-start(f32[3072]{0:T(1024)} %copy-done.60) | copy-start | bytes 36868
  1279.7 141.3 %copy-start.74 = (f32[3072]{0:T(1024)S(1)}, f32[3072]{0:T(1024)}, u32[]{:S(2)}) copy-start(f32[3072]{0:T(1024)} %copy-done.73) | copy-start | bytes 36868
  1279.7 141.3 %copy-start.81 = (f32[768]{0:T(1024)S(1)}, f32[768]{0:T(1024)}, u32[]{:S(2)}) copy-start(f32[768]{0:T(1024)} %copy-done.80) | copy-start | bytes 9220
  1279.7 366.4 %reduce-scatter.14.cloned.1.call-start = ((), (), s32[]{:S(2)}) async-start(), calls=%async_computation.16 | async-start | bytes 2654208 | tf_op jit(solution)/shard_map/reduce_scatter | solution.py:316
  1288.4 395.0 %reduce-scatter.24.cloned.1.call-start = ((), (), s32[]{:S(2)}) async-start(), calls=%async_computation.21 | async-start | bytes 442368
  1443.0 286.1 %reduce-scatter.12.cloned.1.call-start = ((), (), s32[]{:S(2)}) async-start(), calls=%async_computation.15 | async-start | bytes 2654208 | tf_op jit(solution)/shard_map/reduce_scatter | solution.py:314
  1452.8 110.5 %copy-start.90 = (f32[768]{0:T(1024)S(1)}, f32[768]{0:T(1024)}, u32[]{:S(2)}) copy-start(f32[768]{0:T(1024)} %get-tuple-element.387) | copy-start | bytes 9220
  1452.8 110.5 %copy-start.97 = (f32[64]{0:T(128)S(1)}, f32[64]{0:T(128)}, u32[]{:S(2)}) copy-start(f32[64]{0:T(128)} %get-tuple-element.393) | copy-start | bytes 772
  1452.8 327.1 %copy-start.54 = (f32[192,96]{1,0:T(8,128)S(1)}, f32[192,96]{1,0:T(8,128)}, u32[]{:S(2)}) copy-start(f32[192,96]{1,0:T(8,128)} %param.52) | copy-start | bytes 221188
  1452.8 328.7 %copy-start.68 = (f32[2,64,96]{2,1,0:T(8,128)S(1)}, f32[2,64,96]{2,1,0:T(8,128)}, u32[]{:S(2)}) copy-start(f32[2,64,96]{2,1,0:T(8,128)} %param.46) | copy-start | bytes 147460
  1452.8 328.7 %copy-start.79 = (f32[2,64,96]{2,1,0:T(8,128)S(1)}, f32[2,64,96]{2,1,0:T(8,128)}, u32[]{:S(2)}) copy-start(f32[2,64,96]{2,1,0:T(8,128)} %param.47) | copy-start | bytes 147460
  1452.9 330.2 %copy-start.23 = (f32[96,1000]{1,0:T(8,128)S(1)}, f32[96,1000]{1,0:T(8,128)}, u32[]{:S(2)}) copy-start(f32[96,1000]{1,0:T(8,128)} %param.61) | copy-start | bytes 1152004
  1452.9 330.2 %copy-start.55 = (f32[96,1000]{1,0:T(8,128)S(1)}, f32[96,1000]{1,0:T(8,128)}, u32[]{:S(2)}) copy-start(f32[96,1000]{1,0:T(8,128)} %param.62) | copy-start | bytes 1152004
  1452.9 332.6 %copy-start.26 = (f32[768,96]{0,1:T(8,128)S(1)}, f32[768,96]{0,1:T(8,128)}, u32[]{:S(2)}) copy-start(f32[768,96]{0,1:T(8,128)} %param.58) | copy-start | bytes 884740
  1457.4 330.1 %copy-start.28 = (f32[96,768]{1,0:T(8,128)S(1)}, f32[96,768]{1,0:T(8,128)}, u32[]{:S(2)}) copy-start(f32[96,768]{1,0:T(8,128)} %param.55) | copy-start | bytes 884740
  1457.4 332.3 %copy-start.29 = (f32[96,3,192]{2,0,1:T(8,128)S(1)}, f32[96,3,192]{2,0,1:T(8,128)}, u32[]{:S(2)}) copy-start(f32[96,3,192]{2,0,1:T(8,128)} %param.49) | copy-start | bytes 663556
  1457.4 333.3 %copy-start.30 = (f32[768,96]{0,1:T(8,128)S(1)}, f32[768,96]{0,1:T(8,128)}, u32[]{:S(2)}) copy-start(f32[768,96]{0,1:T(8,128)} %param.43) | copy-start | bytes 884740
  1465.8 319.6 %copy-start.31 = (f32[768,96]{0,1:T(8,128)S(1)}, f32[768,96]{0,1:T(8,128)}, u32[]{:S(2)}) copy-start(f32[768,96]{0,1:T(8,128)} %reduce-scatter.18.cloned.1.call-done) | copy-start | bytes 884740
  1511.9 275.7 %copy-start.32 = (f32[96,768]{1,0:T(8,128)S(1)}, f32[96,768]{1,0:T(8,128)}, u32[]{:S(2)}) copy-start(f32[96,768]{1,0:T(8,128)} %reduce-scatter.16.cloned.1.call-done) | copy-start | bytes 884740
  1646.1 143.6 %copy-start.33 = (f32[96,3,192]{2,0,1:T(8,128)S(1)}, f32[96,3,192]{2,0,1:T(8,128)}, u32[]{:S(2)}) copy-start(f32[96,3,192]{2,0,1:T(8,128)} %reduce-scatter.14.cloned.1.call-done) | copy-start | bytes 663556
  1729.1 61.6 %copy-start.34 = (f32[768,96]{0,1:T(8,128)S(1)}, f32[768,96]{0,1:T(8,128)}, u32[]{:S(2)}) copy-start(f32[768,96]{0,1:T(8,128)} %reduce-scatter.12.cloned.1.call-done) | copy-start | bytes 884740
  (75 other events, 595.6 us)
Sparse Core Ops, SparseCore 0:
  10.6 29.3 all-gather.4
  186.1 172.2 all-reduce.5
  360.9 23.0 all-gather.6
  386.3 24.0 all-gather.8
  419.3 171.9 all-reduce.7
  593.6 24.6 all-gather.10
  680.7 171.1 all-reduce.9
  1249.9 170.9 all-reduce.11
  1424.3 41.4 reduce-scatter.17
  1469.4 42.4 reduce-scatter.15
  1515.3 46.2 reduce-scatter.19
  1564.9 34.9 reduce-scatter.21
  1603.6 42.4 reduce-scatter.13
  1649.6 33.8 reduce-scatter.23
  1686.6 42.4 reduce-scatter.11
where the time goes:
time: 1810 us; the launch traced here: 1800 us
  waiting for transfers between devices  910 us (50%)
  matrix products  440 us (24%)
  local copies, waits for them, and re-layouts  173 us (10%)
  other arithmetic  165 us (9%)
  blocking collectives  76.9 us (4%)
  between operations  23.9 us (1%)
    psum x1, waiting for transfers between devices, per_device(): lax.psum(jnp.dot(d_hidden, w_up.T, preferred_element_type=jnp.float32).as...  171 us
    psum x1, waiting for transfers between devices, per_device(): lax.psum(jnp.dot(active_low, w_down, preferred_element_type=jnp.float32)....  171 us
    psum x1, waiting for transfers between devices, per_device(): lax.psum(jnp.dot(attended, w_out, preferred_element_type=jnp.float32).ast...  171 us
    psum x1, waiting for transfers between devices, per_device(): lax.psum(jnp.einsum('tcf,dcf->td', d_joined, w_in, preferred_element_type...  132 us
    dot_general x6, matrix products, backward_block(): jnp.einsum('hqk,qhd->khd', d_scores, query_part, preferred_element_type=j...  81.3 us
    dot_general x6, matrix products, backward_block(): jnp.einsum('hqk,khd->qhd', d_scores, key_rows, preferred_element_type=jnp...  80.3 us
    unnamed x17, waiting for transfers between devices  69.8 us
    dynamic_update_slice x12, local copies, waits for them, and re-layouts, per_device(): lax.map(lambda pack_item: attend_back(*pack_item), (query_low, key_low, v...  59 us
  transfers between devices with their start and end apart: 15, of which 13 were waited for; matrix products, arithmetic and copies ran while one was open for 9% of the time, Pallas kernels for 0%

commit v1 on v0

v1 whole, which is shorter than its diff:
```python
import functools

import jax
import jax.numpy as jnp
from jax import lax
from jax.experimental import pallas as pl
from jax.experimental.pallas import tpu as pltpu
from jax.sharding import PartitionSpec as P

STEP = 10
NORM_EPS = 1e-06
CLIP = 0.05
RATE_BASE = 0.03
RATE_POSITION = 0.2
RATE_MIDDLE = 0.1
RATE_VECTOR = 1.0
DECAY = 0.05
BETA_ONE = 0.5
BETA_TWO = 0.5
ADAM_EPS = 1e-08
SHIFT = -4.0
NEGATIVE = -1e30
APART = 128.0
LOW = jnp.bfloat16
F32 = jnp.float32
VMEM_BYTES = 56 * 1024 * 1024
TAIL_P = 0.3
TAIL = (
    0.1196293,
    0.12075397,
    0.09991341,
    0.12856192,
    -0.05368424,
    0.20635419,
    -0.1572035,
    0.03567488,
)


def mm(left, right):
    return lax.dot_general(left, right, (((1,), (0,)), ((), ())), preferred_element_type=F32)


def mm_nt(left, right):
    return lax.dot_general(left, right, (((1,), (1,)), ((), ())), preferred_element_type=F32)


def split_two(values):
    high = values.astype(LOW)
    return high, (values - high.astype(F32)).astype(LOW)


def split_three(values):
    high = values.astype(LOW)
    rest = values - high.astype(F32)
    middle = rest.astype(LOW)
    return high, middle, (rest - middle.astype(F32)).astype(LOW)


def row_norm(values):
    center = values - jnp.mean(values, axis=-1, keepdims=True)
    inverse = lax.rsqrt(jnp.mean(center * center, axis=-1, keepdims=True) + NORM_EPS)
    return center * inverse, inverse


def row_norm_back(gradient, gain_row, normed, inverse):
    scaled = gradient * gain_row
    return inverse * (
        scaled
        - jnp.mean(scaled, axis=-1, keepdims=True)
        - normed * jnp.mean(scaled * normed, axis=-1, keepdims=True)
    )


def half_mean_matrix(scale):
    row = lax.broadcasted_iota(jnp.int32, (128, 128), 0)
    col = lax.broadcasted_iota(jnp.int32, (128, 128), 1)
    return jnp.where((row >= 64) == (col >= 64), scale, 0.0).astype(LOW)


def half_sum(values, block):
    high, low = split_two(values)
    return mm(high, block) + mm(low, block)


def half_norm(values, block):
    center = values - half_sum(values, block)
    inverse = lax.rsqrt(half_sum(center * center, block) + NORM_EPS)
    return center * inverse, inverse


def half_norm_back(gradient, gain_row, normed, inverse, block):
    scaled = gradient * gain_row
    return inverse * (scaled - half_sum(scaled, block) - normed * half_sum(scaled * normed, block))


def gelu_pair(inner):
    size = jnp.abs(inner)
    near = 1.0 / (1.0 + TAIL_P * size)
    bell = jnp.exp(-0.5 * inner * inner)
    poly = TAIL[-1]
    for factor in TAIL[-2::-1]:
        poly = poly * near + factor
    tail = poly * near * bell
    share = jnp.where(inner >= 0, 1.0 - tail, tail)
    return inner * share, share + inner * bell * 0.3989422804014327


def embed_kernel(pack_ref, pix_ref, coord_ref, wp_ref, win_ref, gain_ref, emb_ref, h1_ref, q_ref, k_ref, v_ref):
    rows = pix_ref.shape[0]
    pixels = pix_ref.shape[1]
    groups = win_ref.shape[0]
    part = win_ref.shape[2] // 3
    spots = (wp_ref.shape[1] - pixels) // 2
    lane = lax.broadcasted_iota(jnp.int32, (rows, 2 * spots), 1)
    hot = ((lane == coord_ref[:, 0:1]) | (lane - spots == coord_ref[:, 1:2])).astype(F32).astype(LOW)
    embedded = mm_nt(pix_ref[...], wp_ref[:, :pixels]) + mm_nt(hot, wp_ref[:, pixels:])
    emb_ref[...] = embedded
    normed, _ = row_norm(embedded)
    first = (normed * gain_ref[0:1]).astype(LOW)
    h1_ref[...] = first
    parts = [mm(first, win_ref[group]) for group in range(groups)]
    q_ref[...] = jnp.concatenate([entry[:, :part] for entry in parts], axis=1)
    k_ref[...] = jnp.concatenate([entry[:, part : 2 * part] for entry in parts], axis=1)
    v_ref[...] = jnp.concatenate([entry[:, 2 * part :].astype(LOW) for entry in parts], axis=1)


def embed_call(pack, pixels, coords, w_pp, w_in, vectors, rows):
    width = vectors.shape[1]
    tile = 256
    steps = rows // tile
    whole2 = lambda i, p: (0, 0)
    tiled = pl.BlockSpec((tile, width), lambda i, p: (i, 0))
    return pl.pallas_call(
        embed_kernel,
        grid_spec=pltpu.PrefetchScalarGridSpec(
            num_scalar_prefetch=1,
            grid=(steps,),
            in_specs=[
                pl.BlockSpec((tile, pixels.shape[1]), lambda i, p: (p[0] * steps + i, 0)),
                pl.BlockSpec((tile, 2), lambda i, p: (p[0] * steps + i, 0)),
                pl.BlockSpec(w_pp.shape, whole2),
                pl.BlockSpec(w_in.shape, lambda i, p: (0, 0, 0)),
                pl.BlockSpec(vectors.shape, whole2),
            ],
            out_specs=[tiled] * 5,
        ),
        out_shape=[
            jax.ShapeDtypeStruct((rows, width), F32),
            jax.ShapeDtypeStruct((rows, width), LOW),
            jax.ShapeDtypeStruct((rows, width), F32),
            jax.ShapeDtypeStruct((rows, width), F32),
            jax.ShapeDtypeStruct((rows, width), LOW),
        ],
        compiler_params=pltpu.CompilerParams(vmem_limit_bytes=VMEM_BYTES),
        name="embed",
    )(pack, pixels, coords, w_pp, w_in, vectors)


def image_marks(bound_ref, rows):
    place = lax.broadcasted_iota(jnp.int32, (rows, 128), 0)
    return (place >= bound_ref[0:1, :]) & (place < bound_ref[1:2, :])


def half_lane(rows):
    lane = lax.broadcasted_iota(jnp.int32, (rows, 128), 1)
    return lane, jnp.where(lane >= 64, lane - 64, lane)


def attend_kernel(q_ref, k_ref, v_ref, gain_ref, bound_ref, o_ref, lse_ref, ka_ref, va_ref, qa_ref):
    rows = q_ref.shape[0]
    tile = 256
    block = half_mean_matrix(1.0 / 64)
    lane, inner = half_lane(rows)
    marks = image_marks(bound_ref, rows)
    one = jnp.where(inner == 8, 1.0, 0.0)
    query_feature = jnp.where(marks, 1.0, one)
    key_feature = jnp.where(marks, APART, -APART * one)
    k_normed, _ = half_norm(k_ref[...], block)
    ka_ref[:, :128] = (k_normed * gain_ref[1:2]).astype(LOW)
    ka_ref[:, 128:] = key_feature.astype(LOW)
    va_ref[:, :128] = v_ref[...]
    va_ref[:, 128:] = jnp.ones((rows, 128), LOW)
    q_normed, _ = half_norm(q_ref[...], block)
    query = (q_normed * gain_ref[0:1]).astype(LOW).astype(F32) * 0.125
    for head in range(2):
        mine = (lane < 64) if head == 0 else (lane >= 64)
        qa_ref[head, :, :128] = jnp.where(mine, query, 0.0).astype(LOW)
        qa_ref[head, :, 128:] = jnp.where(mine, query_feature, 0.0).astype(LOW)
    keys = ka_ref[...]
    values = va_ref[...]
    first = lane[:tile] < 64
    for step in range(rows // tile):
        part = slice(step * tile, (step + 1) * tile)
        outs = []
        for head in range(2):
            score = mm_nt(qa_ref[head, part, :], keys)
            outs.append(mm(jnp.exp(score).astype(LOW), values))
        total = jnp.where(first, outs[0][:, 128:], outs[1][:, 128:])
        o_ref[part, :] = (jnp.where(first, outs[0][:, :128], outs[1][:, :128]) / total).astype(LOW)
        lse_ref[part, :] = jnp.log(total)


def attend_call(q_raw, k_raw, value, gains, bounds):
    rows, width = q_raw.shape
    pair = pl.BlockSpec((rows, 128), lambda j: (0, j))
    small = lambda a: pl.BlockSpec(a.shape, lambda j: (0, 0))
    return pl.pallas_call(
        attend_kernel,
        grid=(width // 128,),
        in_specs=[pair, pair, pair, small(gains), small(bounds)],
        out_specs=[pair, pair],
        out_shape=[
            jax.ShapeDtypeStruct((rows, width), LOW),
            jax.ShapeDtypeStruct((rows, width), F32),
        ],
        scratch_shapes=[
            pltpu.VMEM((rows, 256), LOW),
            pltpu.VMEM((rows, 256), LOW),
            pltpu.VMEM((2, rows, 256), LOW),
        ],
        compiler_params=pltpu.CompilerParams(vmem_limit_bytes=VMEM_BYTES),
        name="attend",
    )(q_raw, k_raw, value, gains, bounds)


def attend_back_kernel(
    q_ref, k_ref, v_ref, o_ref, lse_ref, do_ref, gain_ref, bound_ref,
    dq_ref, dk_ref, dv_ref, dgain_ref,
    ka_ref, va_ref, qa_ref, da_ref, qt_ref, dot_ref, dqs_ref, dkt_ref, dvt_ref,
):
    rows = q_ref.shape[0]
    tile = 256
    block = half_mean_matrix(1.0 / 64)
    block_sum = half_mean_matrix(1.0)
    lane, inner = half_lane(rows)
    marks = image_marks(bound_ref, rows)
    one = jnp.where(inner == 8, 1.0, 0.0)
    three = (inner >= 9) & (inner < 12)
    key_feature = jnp.where(marks, APART, jnp.where(three, 1.0, -APART * one))

    def spread(values):
        high, middle, low = split_three(values)
        return jnp.where(
            inner == 9, high.astype(F32), jnp.where(inner == 10, middle.astype(F32), low.astype(F32))
        )

    query_feature = jnp.where(three, spread(-lse_ref[...]), jnp.where(marks, 1.0, one))
    k_normed, k_inverse = half_norm(k_ref[...], block)
    ka_ref[:, :128] = (k_normed * gain_ref[1:2]).astype(LOW)
    ka_ref[:, 128:] = key_feature.astype(LOW)
    va_ref[:, :128] = v_ref[...]
    va_ref[:, 128:] = jnp.where(three, 1.0, 0.0).astype(LOW)
    q_normed, q_inverse = half_norm(q_ref[...], block)
    query = (q_normed * gain_ref[0:1]).astype(LOW).astype(F32)
    qt_ref[...] = jnp.transpose(query).astype(LOW)
    query = query * 0.125
    above = do_ref[...].astype(F32)
    dot_ref[...] = jnp.transpose(above).astype(LOW)
    inside = half_sum(above * o_ref[...].astype(F32), block_sum)
    above_feature = jnp.where(three, spread(inside * -0.125), 0.0)
    above = above * 0.125
    for head in range(2):
        mine = (lane < 64) if head == 0 else (lane >= 64)
        qa_ref[head, :, :128] = jnp.where(mine, query, 0.0).astype(LOW)
        qa_ref[head, :, 128:] = jnp.where(mine, query_feature, 0.0).astype(LOW)
        da_ref[head, :, :128] = jnp.where(mine, above, 0.0).astype(LOW)
        da_ref[head, :, 128:] = jnp.where(mine, above_feature, 0.0).astype(LOW)
    keys = ka_ref[...]
    values = va_ref[...]
    key_low = ka_ref[:, :128]
    first = lane[:tile] < 64
    for step in range(rows // tile):
        part = slice(step * tile, (step + 1) * tile)
        outs = []
        for head in range(2):
            mine = slice(64 * head, 64 * head + 64)
            prob = jnp.exp(mm_nt(qa_ref[head, part, :], keys))
            d_prob = mm_nt(da_ref[head, part, :], values)
            d_score = (prob * d_prob).astype(LOW)
            outs.append(mm(d_score, key_low))
            d_key = mm(qt_ref[mine, part], d_score)
            d_value = mm(dot_ref[mine, part], prob.astype(LOW))
            if step == 0:
                dkt_ref[mine, :] = d_key
                dvt_ref[mine, :] = d_value
            else:
                dkt_ref[mine, :] += d_key
                dvt_ref[mine, :] += d_value
        dqs_ref[part, :] = jnp.where(first, outs[0], outs[1])
    d_query = dqs_ref[...]
    d_key = jnp.transpose(dkt_ref[...])
    dv_ref[...] = jnp.transpose(dvt_ref[...]).astype(LOW)
    dq_ref[...] = half_norm_back(d_query, gain_ref[0:1], q_normed, q_inverse, block).astype(LOW)
    dk_ref[...] = half_norm_back(d_key, gain_ref[1:2], k_normed, k_inverse, block).astype(LOW)
    dgain_ref[0, 0:1] = jnp.sum(d_query * q_normed, axis=0, keepdims=True)
    dgain_ref[0, 1:2] = jnp.sum(d_key * k_normed, axis=0, keepdims=True)


def attend_back_call(q_raw, k_raw, value, attended, lse, d_attended, gains, bounds):
    rows, width = q_raw.shape
    pairs = width // 128
    pair = pl.BlockSpec((rows, 128), lambda j: (0, j))
    small = lambda a: pl.BlockSpec(a.shape, lambda j: (0, 0))
    low = jax.ShapeDtypeStruct((rows, width), LOW)
    return pl.pallas_call(
        attend_back_kernel,
        grid=(pairs,),
        in_specs=[pair] * 6 + [small(gains), small(bounds)],
        out_specs=[pair, pair, pair, pl.BlockSpec((1, 2, 128), lambda j: (j, 0, 0))],
        out_shape=[low, low, low, jax.ShapeDtypeStruct((pairs, 2, 128), F32)],
        scratch_shapes=[
            pltpu.VMEM((rows, 256), LOW),
            pltpu.VMEM((rows, 256), LOW),
            pltpu.VMEM((2, rows, 256), LOW),
            pltpu.VMEM((2, rows, 256), LOW),
            pltpu.VMEM((128, rows), LOW),
            pltpu.VMEM((128, rows), LOW),
            pltpu.VMEM((rows, 128), F32),
            pltpu.VMEM((128, rows), F32),
            pltpu.VMEM((128, rows), F32),
        ],
        compiler_params=pltpu.CompilerParams(vmem_limit_bytes=VMEM_BYTES),
        name="attend_back",
    )(q_raw, k_raw, value, attended, lse, d_attended, gains, bounds)


def mlp_kernel(o_ref, emb_ref, wout_ref, wup_ref, wdn_ref, vec_ref, x1_ref, h2_ref, act_ref, slope_ref, x2_ref):
    step = pl.program_id(0)
    rows, _ = o_ref.shape
    groups, _, part = wout_ref.shape
    tile = 256

    @pl.when(step == 0)
    def _():
        for at in range(rows // tile):
            span = slice(at * tile, (at + 1) * tile)
            branch = mm_nt(o_ref[span, :part], wout_ref[0])
            for group in range(1, groups):
                branch += mm_nt(o_ref[span, group * part : (group + 1) * part], wout_ref[group])
            middle = emb_ref[span, :] + branch
            x1_ref[span, :] = middle
            x2_ref[span, :] = middle
            normed, _ = row_norm(middle)
            h2_ref[span, :] = (normed * vec_ref[1:2]).astype(LOW)

    for at in range(rows // tile):
        span = slice(at * tile, (at + 1) * tile)
        active, slope = gelu_pair(mm(h2_ref[span, :], wup_ref[0]))
        active = active.astype(LOW)
        act_ref[span, :] = active
        slope_ref[span, :] = slope.astype(LOW)
        x2_ref[span, :] += mm_nt(active, wdn_ref[0])


def mlp_call(attended, embedded, w_out, w_up, w_dn, vectors):
    rows, width = embedded.shape
    groups, _, per = w_up.shape
    chunk = per // 2
    hidden = groups * per
    whole = lambda a: pl.BlockSpec(a.shape, lambda j: (0,) * a.ndim)
    weight = pl.BlockSpec((1, width, chunk), lambda j: (j // 2, 0, j % 2))
    full = pl.BlockSpec((rows, width), lambda j: (0, 0))
    piece = pl.BlockSpec((rows, chunk), lambda j: (0, j))
    return pl.pallas_call(
        mlp_kernel,
        grid=(hidden // chunk,),
        in_specs=[whole(attended), whole(embedded), whole(w_out), weight, weight, whole(vectors)],
        out_specs=[full, full, piece, piece, full],
        out_shape=[
            jax.ShapeDtypeStruct((rows, width), F32),
            jax.ShapeDtypeStruct((rows, width), LOW),
            jax.ShapeDtypeStruct((rows, hidden), LOW),
            jax.ShapeDtypeStruct((rows, hidden), LOW),
            jax.ShapeDtypeStruct((rows, width), F32),
        ],
        compiler_params=pltpu.CompilerParams(vmem_limit_bytes=VMEM_BYTES),
        name="mlp",
    )(attended, embedded, w_out, w_up, w_dn, vectors)


def pool_kernel(
    pack_ref, x2_ref, label_ref, wcls_ref, vec_ref, bound_ref, valid_ref,
    dx2_ref, dcls_ref, loss_ref, dvec_ref,
    norm_ref, inv_ref,
    *, images, image_count,
):
    rows, width = x2_ref.shape
    tile = 256
    root = width**0.5
    gain = vec_ref[2:3]
    query = vec_ref[3:4]
    lane = lax.broadcasted_iota(jnp.int32, (rows, 128), 1)
    marks = image_marks(bound_ref, rows) & (lane < 64)
    logits = []
    for at in range(rows // tile):
        span = slice(at * tile, (at + 1) * tile)
        normed, inverse = row_norm(x2_ref[span, :])
        norm_ref[span, :] = normed
        inv_ref[span, :] = jnp.broadcast_to(inverse, (tile, 128))
        logits.append(jnp.sum(normed * gain * query, axis=-1, keepdims=True) / root)
    logit = jnp.concatenate(logits, axis=0)
    masked = jnp.where(marks, logit, NEGATIVE)
    grown = jnp.exp(masked - jnp.max(masked, axis=0, keepdims=True))
    shares = jnp.where(marks, grown / jnp.sum(grown, axis=0, keepdims=True), 0.0)
    weight = jnp.sum(shares, axis=-1, keepdims=True)
    member = jnp.transpose(marks.astype(F32))[:16].astype(LOW)
    pooled = jnp.zeros((16, width), F32)
    for at in range(rows // tile):
        span = slice(at * tile, (at + 1) * tile)
        for entry in split_three(norm_ref[span, :] * gain * weight[span]):
            pooled += mm(member[:, span], entry)
    pooled_low = pooled.astype(LOW)
    scores = mm(pooled_low, wcls_ref[...])[:images] + SHIFT
    target = label_ref[...].astype(F32)
    valid = valid_ref[0, 0]
    soft = jnp.maximum(scores, 0.0) + jnp.log1p(jnp.exp(-jnp.abs(scores)))
    loss_rows = jnp.sum(soft - target * scores, axis=-1, keepdims=True)
    loss_ref[...] = jnp.broadcast_to(jnp.sum(loss_rows, axis=0, keepdims=True) * valid, loss_ref.shape)
    d_score = (1.0 / (1.0 + jnp.exp(-scores)) - target) / image_count * valid
    d_score = jnp.concatenate([d_score, jnp.zeros((16 - images, d_score.shape[1]), F32)], axis=0).astype(LOW)
    dcls_ref[...] = mm(jnp.transpose(pooled).astype(LOW), d_score).astype(LOW)
    d_pooled = mm_nt(d_score, wcls_ref[...])[:images]
    parts = jnp.concatenate(
        [entry.astype(F32) for entry in split_three(d_pooled)]
        + [jnp.zeros((128 - 3 * images, width), F32)],
        axis=0,
    ).astype(LOW)
    marks_f = marks.astype(F32)
    thrice = (
        marks_f + pltpu.roll(marks_f, images, 1) + pltpu.roll(marks_f, 2 * images, 1)
    ).astype(LOW)
    d_weights = []
    for at in range(rows // tile):
        span = slice(at * tile, (at + 1) * tile)
        spread = mm(thrice[span], parts)
        dx2_ref[span, :] = spread
        d_weights.append(jnp.sum(spread * (norm_ref[span, :] * gain), axis=-1, keepdims=True))
    d_weight = jnp.concatenate(d_weights, axis=0)
    inside = jnp.sum(shares * d_weight, axis=0, keepdims=True)
    d_logit = weight * (d_weight - jnp.sum(marks_f * inside, axis=-1, keepdims=True))
    gain_sum = jnp.zeros((1, width), F32)
    query_sum = jnp.zeros((1, width), F32)
    for at in range(rows // tile):
        span = slice(at * tile, (at + 1) * tile)
        normed = norm_ref[span, :]
        inverse = inv_ref[span, 0:1]
        d_last = dx2_ref[span, :] * weight[span] + d_logit[span] * (query / root)
        gain_sum += jnp.sum(d_last * normed, axis=0, keepdims=True)
        query_sum += jnp.sum(d_logit[span] * normed, axis=0, keepdims=True)
        dx2_ref[span, :] = row_norm_back(d_last, gain, normed, inverse)
    dvec_ref[0:1, :] = gain_sum
    dvec_ref[1:2, :] = query_sum * gain / root


def pool_call(pack, x2, labels, w_cls, vectors, bounds, valid, images, image_count):
    rows, width = x2.shape
    classes = labels.shape[1]
    whole = lambda a: pl.BlockSpec(a.shape, lambda j, p: (0,) * a.ndim)
    full = lambda *shape: pl.BlockSpec(shape, lambda j, p: (0,) * len(shape))
    return pl.pallas_call(
        functools.partial(pool_kernel, images=images, image_count=image_count),
        grid_spec=pltpu.PrefetchScalarGridSpec(
            num_scalar_prefetch=1,
            grid=(1,),
            in_specs=[
                whole(x2),
                pl.BlockSpec((images, classes), lambda j, p: (p[0], 0)),
                whole(w_cls),
                whole(vectors),
                whole(bounds),
                pl.BlockSpec(memory_space=pltpu.SMEM),
            ],
            out_specs=[full(rows, width), full(width, classes), full(8, 128), full(2, width)],
            scratch_shapes=[pltpu.VMEM((rows, width), F32), pltpu.VMEM((rows, 128), F32)],
        ),
        out_shape=[
            jax.ShapeDtypeStruct((rows, width), F32),
            jax.ShapeDtypeStruct((width, classes), LOW),
            jax.ShapeDtypeStruct((8, 128), F32),
            jax.ShapeDtypeStruct((2, width), F32),
        ],
        compiler_params=pltpu.CompilerParams(vmem_limit_bytes=VMEM_BYTES),
        name="pool",
    )(pack, x2, labels, w_cls, vectors, bounds, valid)


def mlp_back_kernel(
    dx2_ref, act_ref, slope_ref, h2_ref, x1_ref, o_ref, wout_ref, wup_ref, wdn_ref, vec_ref,
    ddn_ref, dup_ref, dout_ref, do_ref, dmid_ref, dvec_ref,
    low_ref, lowt_ref, h2t_ref, acc_ref, dh_ref,
):
    step = pl.program_id(0)
    rows, width = dx2_ref.shape
    groups, _, part = wout_ref.shape
    tile = 256

    @pl.when(step == 0)
    def _():
        for at in range(rows // tile):
            span = slice(at * tile, (at + 1) * tile)
            values = dx2_ref[span, :]
            low_ref[span, :] = values.astype(LOW)
            lowt_ref[:, span] = jnp.transpose(values).astype(LOW)
            h2t_ref[:, span] = jnp.transpose(h2_ref[span, :].astype(F32)).astype(LOW)
            acc_ref[span, :] = jnp.zeros((tile, width), F32)

    for at in range(rows // tile):
        span = slice(at * tile, (at + 1) * tile)
        d_hidden = (mm(low_ref[span, :], wdn_ref[0]) * slope_ref[span, :].astype(F32)).astype(LOW)
        dh_ref[span, :] = d_hidden
        acc_ref[span, :] += mm_nt(d_hidden, wup_ref[0])
    for at in range(width // tile):
        span = slice(at * tile, (at + 1) * tile)
        ddn_ref[0, span, :] = mm(lowt_ref[span, :], act_ref[...]).astype(LOW)
        dup_ref[0, span, :] = mm(h2t_ref[span, :], dh_ref[...]).astype(LOW)

    @pl.when(step == pl.num_programs(0) - 1)
    def _():
        gain = vec_ref[1:2]
        gain_sum = jnp.zeros((1, width), F32)
        for at in range(rows // tile):
            span = slice(at * tile, (at + 1) * tile)
            normed, inverse = row_norm(x1_ref[span, :])
            d_second = acc_ref[span, :]
            gain_sum += jnp.sum(d_second * normed, axis=0, keepdims=True)
            d_middle = dx2_ref[span, :] + row_norm_back(d_second, gain, normed, inverse)
            dmid_ref[span, :] = d_middle
            low = d_middle.astype(LOW)
            lowt_ref[:, span] = jnp.transpose(d_middle).astype(LOW)
            do_ref[span, :] = jnp.concatenate(
                [mm(low, wout_ref[group]) for group in range(groups)], axis=1
            ).astype(LOW)
        dvec_ref[...] = gain_sum
        for group in range(groups):
            piece = o_ref[:, group * part : (group + 1) * part]
            for at in range(width // tile):
                span = slice(at * tile, (at + 1) * tile)
                dout_ref[group, span, :] = mm(lowt_ref[span, :], piece).astype(LOW)


def mlp_back_call(dx2, active, slope, h2, x1, attended, w_out, w_up, w_dn, vectors):
    rows, width = dx2.shape
    groups, _, per = w_up.shape
    chunk = per // 2
    hidden = groups * per
    whole = lambda a: pl.BlockSpec(a.shape, lambda j: (0,) * a.ndim, pipeline_mode=pl.Buffered(1))
    weight = pl.BlockSpec((1, width, chunk), lambda j: (j // 2, 0, j % 2))
    piece = pl.BlockSpec((rows, chunk), lambda j: (0, j))
    full = lambda *shape: pl.BlockSpec(shape, lambda j: (0,) * len(shape))
    return pl.pallas_call(
        mlp_back_kernel,
        grid=(hidden // chunk,),
        in_specs=[
            whole(dx2), piece, piece, whole(h2), whole(x1), whole(attended), whole(w_out),
            weight, weight, whole(vectors),
        ],
        out_specs=[weight, weight, full(*w_out.shape), full(rows, width), full(rows, width), full(1, width)],
        out_shape=[
            jax.ShapeDtypeStruct(w_dn.shape, LOW),
            jax.ShapeDtypeStruct(w_up.shape, LOW),
            jax.ShapeDtypeStruct(w_out.shape, LOW),
            jax.ShapeDtypeStruct((rows, width), LOW),
            jax.ShapeDtypeStruct((rows, width), F32),
            jax.ShapeDtypeStruct((1, width), F32),
        ],
        scratch_shapes=[
            pltpu.VMEM((rows, width), LOW),
            pltpu.VMEM((width, rows), LOW),
            pltpu.VMEM((width, rows), LOW),
            pltpu.VMEM((rows, width), F32),
            pltpu.VMEM((rows, chunk), LOW),
        ],
        compiler_params=pltpu.CompilerParams(vmem_limit_bytes=VMEM_BYTES),
        name="mlp_back",
    )(dx2, active, slope, h2, x1, attended, w_out, w_up, w_dn, vectors)


def embed_back_kernel(
    pack_ref, dq_ref, dk_ref, dv_ref, h1_ref, emb_ref, dmid_ref, pix_ref, coord_ref, win_ref, vec_ref,
    din_ref, dpp_ref, dvec_ref,
    h1t_ref, join_ref, acc_ref,
):
    step = pl.program_id(0)
    rows, width = h1_ref.shape
    groups = pl.num_programs(0)
    part = win_ref.shape[2] // 3
    tile = 256

    @pl.when(step == 0)
    def _():
        for at in range(rows // tile):
            span = slice(at * tile, (at + 1) * tile)
            h1t_ref[:, span] = jnp.transpose(h1_ref[span, :].astype(F32)).astype(LOW)
            acc_ref[span, :] = jnp.zeros((tile, width), F32)

    for group in range(width // part):

        @pl.when(step == group)
        def _():
            mine = slice(group * part, (group + 1) * part)
            join_ref[...] = jnp.concatenate([dq_ref[:, mine], dk_ref[:, mine], dv_ref[:, mine]], axis=1)

    for at in range(rows // tile):
        span = slice(at * tile, (at + 1) * tile)
        acc_ref[span, :] += mm_nt(join_ref[span, :], win_ref[0])
    for at in range(width // tile):
        span = slice(at * tile, (at + 1) * tile)
        din_ref[0, span, :] = mm(h1t_ref[span, :], join_ref[...]).astype(LOW)

    @pl.when(step == groups - 1)
    def _():
        gain = vec_ref[0:1]
        pixels = pix_ref.shape[1]
        spots = (dpp_ref.shape[1] - pixels) // 2
        gain_sum = jnp.zeros((1, width), F32)
        for at in range(rows // tile):
            span = slice(at * tile, (at + 1) * tile)
            normed, inverse = row_norm(emb_ref[span, :])
            d_first = acc_ref[span, :]
            gain_sum += jnp.sum(d_first * normed, axis=0, keepdims=True)
            d_embed = dmid_ref[span, :] + row_norm_back(d_first, gain, normed, inverse)
            h1t_ref[:, span] = jnp.transpose(d_embed).astype(LOW)
        dvec_ref[...] = gain_sum
        lane = lax.broadcasted_iota(jnp.int32, (rows, 2 * spots), 1)
        hot = ((lane == coord_ref[:, 0:1]) | (lane - spots == coord_ref[:, 1:2])).astype(F32).astype(LOW)
        for at in range(width // tile):
            span = slice(at * tile, (at + 1) * tile)
            dpp_ref[span, :pixels] = mm(h1t_ref[span, :], pix_ref[...]).astype(LOW)
            dpp_ref[span, pixels:] = mm(h1t_ref[span, :], hot).astype(LOW)


def embed_back_call(pack, dq, dk, dv, h1, embedded, d_middle, pixels, coords, w_in, w_pp_shape, vectors):
    rows, width = h1.shape
    groups = w_in.shape[0]
    whole = lambda a: pl.BlockSpec(a.shape, lambda j, p: (0,) * a.ndim, pipeline_mode=pl.Buffered(1))
    full = lambda *shape: pl.BlockSpec(shape, lambda j, p: (0,) * len(shape))
    weight = pl.BlockSpec((1,) + w_in.shape[1:], lambda j, p: (j, 0, 0))
    return pl.pallas_call(
        embed_back_kernel,
        grid_spec=pltpu.PrefetchScalarGridSpec(
            num_scalar_prefetch=1,
            grid=(groups,),
            in_specs=[
                whole(dq), whole(dk), whole(dv), whole(h1), whole(embedded), whole(d_middle),
                pl.BlockSpec((rows, pixels.shape[1]), lambda j, p: (p[0], 0)),
                pl.BlockSpec((rows, 2), lambda j, p: (p[0], 0)),
                weight,
                whole(vectors),
            ],
            out_specs=[weight, full(*w_pp_shape), full(1, width)],
            scratch_shapes=[
                pltpu.VMEM((width, rows), LOW),
                pltpu.VMEM((rows, w_in.shape[2]), LOW),
                pltpu.VMEM((rows, width), F32),
            ],
        ),
        out_shape=[
            jax.ShapeDtypeStruct(w_in.shape, LOW),
            jax.ShapeDtypeStruct(w_pp_shape, LOW),
            jax.ShapeDtypeStruct((1, width), F32),
        ],
        compiler_params=pltpu.CompilerParams(vmem_limit_bytes=VMEM_BYTES),
        name="embed_back",
    )(pack, dq, dk, dv, h1, embedded, d_middle, pixels, coords, w_in, vectors)


def pack_step(pack, valid, pixels, coords, lengths, labels, weights, vectors, head_gains, image_count):
    w_pp, w_in, w_out, w_up, w_dn, w_cls = weights
    packs, images = lengths.shape
    rows = pixels.shape[0] // packs
    mine = lax.dynamic_index_in_dim(lengths, pack[0], 0, keepdims=False)
    ends = jnp.cumsum(mine)
    fill = jnp.full((64 - images,), 1 << 30, jnp.int32)
    starts = jnp.concatenate([ends - mine, fill])
    ends = jnp.concatenate([ends, fill])
    bounds = jnp.stack([jnp.tile(starts, 2), jnp.tile(ends, 2)])
    gains = jnp.tile(head_gains, (1, 2))
    places = coords.T
    embedded, h1, q_raw, k_raw, value = embed_call(pack, pixels, places, w_pp, w_in, vectors, rows)
    attended, lse = attend_call(q_raw, k_raw, value, gains, bounds)
    x1, h2, active, slope, x2 = mlp_call(attended, embedded, w_out, w_up, w_dn, vectors)
    dx2, d_cls, loss, dvec_pool = pool_call(
        pack, x2, labels, w_cls, vectors, bounds, valid, images, image_count
    )
    d_dn, d_up, d_out, d_attended, d_middle, dvec_two = mlp_back_call(
        dx2, active, slope, h2, x1, attended, w_out, w_up, w_dn, vectors
    )
    dq, dk, dv, d_gain = attend_back_call(q_raw, k_raw, value, attended, lse, d_attended, gains, bounds)
    d_in, d_pp, dvec_one = embed_back_call(
        pack, dq, dk, dv, h1, embedded, d_middle, pixels, places, w_in, w_pp.shape, vectors
    )
    d_vectors = jnp.concatenate([dvec_one, dvec_two, dvec_pool], axis=0)
    d_gains = jnp.sum(d_gain.reshape(-1, 2, 2, 64), axis=(0, 2))
    return (d_pp, d_in, d_out, d_up, d_dn, d_cls), d_vectors, d_gains, loss[0, 0]


def adam(master, first_moment, second_moment, gradient, clip_scale, rate, decay_rate):
    gradient = gradient * clip_scale
    first_new = BETA_ONE * first_moment + (1 - BETA_ONE) * gradient
    second_new = BETA_TWO * second_moment + (1 - BETA_TWO) * gradient * gradient
    update = (
        first_new / (1 - BETA_ONE**STEP) / (jnp.sqrt(second_new / (1 - BETA_TWO**STEP)) + ADAM_EPS)
    )
    return (master - rate * (update + decay_rate * master), first_new, second_new)


def squared(entry):
    return jnp.sum(entry * entry)


def per_device(
    pixels, coords, lengths, labels,
    patch_table, patch_first, patch_second,
    position_table, position_first, position_second,
    attend_in, attend_in_first, attend_in_second,
    attend_out, attend_out_first, attend_out_second,
    expand, expand_first, expand_second,
    shrink, shrink_first, shrink_second,
    classify, classify_first, classify_second,
    vectors, vectors_first, vectors_second,
    head_gains, head_gains_first, head_gains_second,
):
    packs, images = lengths.shape
    members = lax.axis_size("tensor")
    width = vectors.shape[1]
    share = attend_in.shape[0]
    seat = lax.axis_index("tensor")
    pack = jnp.minimum(seat, packs - 1).astype(jnp.int32)[None]
    valid = (seat < packs).astype(F32).reshape(1, 1)
    image_count = images * packs * lax.axis_size("dp")
    shards = (
        jnp.concatenate(
            [patch_table.T, jnp.transpose(position_table, (2, 0, 1)).reshape(share, -1)], axis=1
        ).astype(LOW),
        attend_in.reshape(share, -1).astype(LOW),
        attend_out.T.astype(LOW),
        expand.astype(LOW),
        shrink.T.astype(LOW),
        classify.astype(LOW),
    )
    both = ("tensor", "dp")

    def gather(shard):
        return lax.all_gather(shard, both, axis=0, tiled=True).reshape(members, width, -1)

    weights = (
        lax.all_gather(shards[0], "dp", axis=0, tiled=True),
        gather(shards[1]),
        gather(shards[2]),
        gather(shards[3]),
        gather(shards[4]),
        lax.all_gather(shards[5], "dp", axis=0, tiled=True),
    )
    grads, grad_vectors, grad_gains, loss_local = pack_step(
        pack, valid, pixels, coords, lengths, labels, weights, vectors, head_gains, image_count
    )
    grad_vectors, grad_gains, loss_total = lax.psum((grad_vectors, grad_gains, loss_local), both)

    def scatter(grad):
        return lax.psum_scatter(
            grad.reshape(members * width, -1), both, scatter_dimension=0, tiled=True
        ).astype(F32)

    def scatter_whole(grad):
        return lax.psum(lax.psum_scatter(grad, "dp", scatter_dimension=0, tiled=True), "tensor").astype(F32)

    share_pp = scatter_whole(grads[0])
    share_in, share_out, share_up, share_dn = (scatter(entry) for entry in grads[1:5])
    share_cls = scatter_whole(grads[5])
    leader = (seat == 0).astype(F32)
    split_squares = squared(share_in) + squared(share_out) + squared(share_up) + squared(share_dn)
    whole_squares = squared(share_pp) + squared(share_cls)
    squares = lax.psum(split_squares + leader * whole_squares, both)
    grad_norm = jnp.sqrt(squares + squared(grad_vectors) + squared(grad_gains))
    clip_scale = CLIP / jnp.maximum(grad_norm, CLIP)
    pixel_width = patch_table.shape[0]
    share_patch = share_pp[:, :pixel_width].T
    share_pos = jnp.transpose(
        share_pp[:, pixel_width:].reshape(share, position_table.shape[0], position_table.shape[1]), (1, 2, 0)
    )
    results = (
        adam(patch_table, patch_first, patch_second, share_patch, clip_scale, RATE_BASE, DECAY),
        adam(position_table, position_first, position_second, share_pos, clip_scale, RATE_POSITION, DECAY),
        adam(
            attend_in, attend_in_first, attend_in_second,
            share_in.reshape(attend_in.shape), clip_scale, RATE_BASE, DECAY,
        ),
        adam(attend_out, attend_out_first, attend_out_second, share_out.T, clip_scale, RATE_MIDDLE, DECAY),
        adam(expand, expand_first, expand_second, share_up, clip_scale, RATE_BASE, DECAY),
        adam(shrink, shrink_first, shrink_second, share_dn.T, clip_scale, RATE_BASE, DECAY),
        adam(classify, classify_first, classify_second, share_cls, clip_scale, RATE_MIDDLE, DECAY),
        adam(vectors, vectors_first, vectors_second, grad_vectors, clip_scale, RATE_VECTOR, 0.0),
        adam(head_gains, head_gains_first, head_gains_second, grad_gains, clip_scale, RATE_VECTOR, 0.0),
    )
    return tuple(entry for group in results for entry in group) + (loss_total, grad_norm)


def solution(mesh):
    data = P("dp", None)
    in_specs = (
        (data, P(None, "dp"), data, data)
        + (P(None, "dp"),) * 3
        + (P(None, None, "dp"),) * 3
        + (P("dp", None, "tensor"),) * 3
        + (P("tensor", "dp"),) * 3
        + (P("dp", "tensor"),) * 3
        + (P("tensor", "dp"),) * 3
        + (data,) * 3
        + (P(),) * 6
    )
    out_specs = in_specs[4:] + (P(), P())
    return jax.shard_map(per_device, mesh=mesh, in_specs=in_specs, out_specs=out_specs, check_vma=False)
```

time: 1810 us -> 1080 us (0.60)
  matrix products: 440 us -> 0 us
  Pallas kernels: 0 us -> 198 us
  local copies, waits for them, and re-layouts: 173 us -> 12 us
  other arithmetic: 165 us -> 26.3 us
  waiting for transfers between devices: 910 us -> 772 us
  blocking collectives: 76.9 us -> 40.6 us
    psum x4 -> x1, waiting for transfers between devices: 645 us -> 36.4 us  [scatter_whole(): lax.psum(lax.psum_scatter(grad, 'dp', scatter_dimension=0, tiled=True), '...]
    dot_general x64 -> x0, matrix products: 431 us -> none  [the longest x6 81.3 us: backward_block(): jnp.einsum('hqk,qhd->khd', d_scores, query_part, preferred_element_type=j...]
    all_gather x4 -> x6, waiting for transfers between devices: 6.4 us -> 234 us  [the longest x4 216 us: gather(): lax.all_gather(shard, both, axis=0, tiled=True).reshape(members, width, -1)]
    pallas_call x0 -> x7, Pallas kernels: none -> 198 us  [the longest x1 47.8 us: attend_back_call(): pl.pallas_call(attend_back_kernel, grid=(pairs,), in_specs=[pair] * 6 + [...]
    unnamed x17 -> x15, waiting for transfers between devices: 69.8 us -> 206 us
    reduce_scatter x5 -> x4, waiting for transfers between devices: 189 us -> 296 us  [the longest x2 218 us: scatter(): lax.psum_scatter(grad.reshape(members * width, -1), both, scatter_dimensi...]
    reduce_sum x22 -> x2, other arithmetic: 89.9 us -> 0.04 us  [pack_step(): d_gains = jnp.sum(d_gain.reshape(-1, 2, 2, 64), axis=(0, 2))]
    dynamic_update_slice x18 -> x0, local copies, waits for them, and re-layouts: 65 us -> none  [the longest x12 59 us: per_device(): lax.map(lambda pack_item: attend_back(*pack_item), (query_low, key_low, v...]
  transfers between devices with their start and end apart: 15 -> 13, of which waited for: 13 -> 12; matrix products, arithmetic and copies ran while one was open for 9% -> 2% of each run, Pallas kernels for 0% -> 7%
where the time goes in v1:
time: 1080 us; the launch traced here: 1070 us
  waiting for transfers between devices  772 us (71%)
  Pallas kernels  198 us (18%)
  blocking collectives  40.6 us (4%)
  other arithmetic  26.3 us (2%)
  between operations  21.7 us (2%)
  local copies, waits for them, and re-layouts  12 us (1%)
    reduce_scatter x2, waiting for transfers between devices, scatter(): lax.psum_scatter(grad.reshape(members * width, -1), both, scatter_dimensi...  218 us
    all_gather x4, waiting for transfers between devices, gather(): lax.all_gather(shard, both, axis=0, tiled=True).reshape(members, width, -1)  216 us
    unnamed x15, waiting for transfers between devices  206 us
    reduce_scatter x2, waiting for transfers between devices, scatter_whole(): lax.psum_scatter(grad, 'dp', scatter_dimension=0, tiled=True)  77.2 us
    pallas_call x1, Pallas kernels, attend_back_call(): pl.pallas_call(attend_back_kernel, grid=(pairs,), in_specs=[pair] * 6 + [...  47.8 us
    pallas_call x1, Pallas kernels, mlp_back_call(): pl.pallas_call(mlp_back_kernel, grid=(hidden // chunk,), in_specs=[whole(...  43.6 us
    psum x1, blocking collectives, per_device(): squares = lax.psum(split_squares + leader * whole_squares, both)  40.6 us
    psum x1, waiting for transfers between devices, scatter_whole(): lax.psum(lax.psum_scatter(grad, 'dp', scatter_dimension=0, tiled=True), '...  36.4 us
  transfers between devices with their start and end apart: 13, of which 12 were waited for; matrix products, arithmetic and copies ran while one was open for 2% of the time, Pallas kernels for 7%

profile of v1, /device:TPU:0, one launch (start us, length us, event | category | flops | bytes accessed | tf_op | source)
XLA Modules:
  0.0 1071.1 jit_solution(5700015715927119636)
XLA Ops:
  7.3 0.9 convert.11
  8.3 1.0 convert_bitcast_fusion.1
  9.3 0.7 pad_maximum_fusion
  10.1 1.0 convert_element_type.45
  11.2 0.8 copy.98
  12.1 1.6 copy.99
  13.8 1.6 convert_element_type.49
  16.2 0.7 convert_element_type.52
  17.0 1.7 copy.95
  20.4 17.8 %all-gather.7.cloned.1.call-done.wp_ref = bf16[768,896]{1,0:T(8,128)(2,1)} async-done(((bf16[96,896]{1,0:T(8,128)(2,1)}), bf16[768,896]{1,0:T(8,128)(2,1)}) %all-gather.7.cloned.1.call-update) | async-done | bytes 1376272 | tf_op jit(solution)/shard_map/all_gather | solution.py:748
  38.2 64.7 %all-gather.9.cloned.1.call-done = bf16[3072,576]{1,0:T(8,128)(2,1)} async-done(((bf16[96,576]{1,0:T(8,128)(2,1)}), bf16[3072,576]{1,0:T(8,128)(2,1)}) %all-gather.9.cloned.1.call-update) | async-done | bytes 3538960 | tf_op jit(solution)/shard_map/all_gather | solution.py:745
  102.9 14.1 %embed.1 = (f32[1024,768]{1,0:T(8,128)}, bf16[1024,768]{1,0:T(8,128)(2,1)}, f32[1024,768]{1,0:T(8,128)}, f32[1024,768]{1,0:T(8,128)}, bf16[1024,768]{1,0:T(8,128)(2,1)}) custom-call(s32[1]{0:T(128)} %bitcast.2.pack_ref, bf16[3072,768]{1,0:T(8,128)(2,1)} %pix_ref.3, s32[3072,2]{1,0:T(8,128)} %bitcast.69, ...), custom_call_target="tpu_custom_call" | custom-call | tf_op jit(solution)/shard_map/embed/pallas_call | solution.py:134
  117.0 23.6 %attend.1 = (bf16[1024,768]{1,0:T(8,128)(2,1)}, f32[1024,768]{1,0:T(8,128)}) custom-call(f32[1024,768]{1,0:T(8,128)} %get-tuple-element.58.q_ref, f32[1024,768]{1,0:T(8,128)} %get-tuple-element.59.k_ref, bf16[1024,768]{1,0:T(8,128)(2,1)} %get-tuple-element.60.v_ref, f32[2,128]{1,0:T(2,128)} %tile.9.gain_ref, s32[2,128]{1,0:T(2,128)} %pad_add_fusion.bound_ref), custom_call_target="tpu_custom_call" | custom-call | tf_op jit(solution)/shard_map/attend/pallas_call | solution.py:208
  140.6 19.4 %all-gather.11.cloned.1.call-done = bf16[3072,192]{1,0:T(8,128)(2,1)} async-done(((bf16[96,192]{1,0:T(8,128)(2,1)}), bf16[3072,192]{1,0:T(8,128)(2,1)}) %all-gather.11.cloned.1.call-update) | async-done | bytes 1179664 | tf_op jit(solution)/shard_map/all_gather | solution.py:745
  160.0 65.9 %all-gather.13.cloned.1.call-done = bf16[3072,768]{1,0:T(8,128)(2,1)} async-done(((bf16[96,768]{1,0:T(8,128)(2,1)}), bf16[3072,768]{1,0:T(8,128)(2,1)}) %all-gather.13.cloned.1.call-update) | async-done | bytes 4718608 | tf_op jit(solution)/shard_map/all_gather | solution.py:745
  225.9 65.8 %all-gather.15.cloned.1.call-done = bf16[3072,768]{1,0:T(8,128)(2,1)} async-done(((bf16[96,768]{1,0:T(8,128)(2,1)}), bf16[3072,768]{1,0:T(8,128)(2,1)}) %all-gather.15.cloned.1.call-update) | async-done | bytes 4718608 | tf_op jit(solution)/shard_map/all_gather | solution.py:745
  291.7 34.1 %mlp.1 = (f32[1024,768]{1,0:T(8,128)}, bf16[1024,768]{1,0:T(8,128)(2,1)}, bf16[1024,3072]{1,0:T(8,128)(2,1)}, bf16[1024,3072]{1,0:T(8,128)(2,1)}, f32[1024,768]{1,0:T(8,128)}) custom-call(bf16[1024,768]{1,0:T(8,128)(2,1)} %get-tuple-element.61.o_ref, f32[1024,768]{1,0:T(8,128)} %get-tuple-element.63.emb_ref, bf16[4,768,192]{2,1,0:T(8,128)(2,1)} %bitcast.71, ...), custom_call_target="tpu_custom_call" | custom-call | tf_op jit(solution)/shard_map/mlp/pallas_call | solution.py:365
  325.8 11.1 %pool.1 = (f32[1024,768]{1,0:T(8,128)}, bf16[768,1000]{1,0:T(8,128)(2,1)}, f32[8,128]{1,0:T(8,128)}, f32[2,768]{1,0:T(2,128)}) custom-call(s32[1]{0:T(128)} %bitcast.2.pack_ref, f32[1024,768]{1,0:T(8,128)} %get-tuple-element.64.x2_ref, s32[24,1000]{1,0:T(8,128)} %label_ref.1, bf16[768,1000]{1,0:T(8,128)(2,1)} %all-gather.17.cloned.1.call-done.wcls_ref, ...), custom_call_target="tpu_custom_call" | custom-call | tf_op jit(solution)/shard_map/pool/pallas_call | solution.py:461
  336.9 43.6 %mlp_back.1 = (bf16[4,768,768]{2,1,0:T(8,128)(2,1)}, bf16[4,768,768]{2,1,0:T(8,128)(2,1)}, bf16[4,768,192]{2,1,0:T(8,128)(2,1)}, bf16[1024,768]{1,0:T(8,128)(2,1...) custom-call(f32[1024,768]{1,0:T(8,128)} %get-tuple-element.65.dx2_ref, bf16[1024,3072]{1,0:T(8,128)(2,1)} %get-tuple-element.66.act_ref, ...), custom_call_target="tpu_custom_call" | custom-call | tf_op jit(solution)/shard_map/mlp_back/pallas_call | solution.py:551
  380.5 47.8 %attend_back.1 = (bf16[1024,768]{1,0:T(8,128)(2,1)}, bf16[1024,768]{1,0:T(8,128)(2,1)}, bf16[1024,768]{1,0:T(8,128)(2,1)}, f32[6,2,128]{2,1,0:T(2,128)}) custom-call(f32[1024,768]{1,0:T(8,128)} %get-tuple-element.58.q_ref, f32[1024,768]{1,0:T(8,128)} %get-tuple-element.59.k_ref, bf16[1024,768]{1,0:T(8,128)(2,1)} %get-tuple-element.60.v_ref, ...), custom_call_target="tpu_custom_call" | custom-call | tf_op jit(solution)/shard_map/attend_back/pallas_call | solution.py:306
  428.2 23.7 %embed_back.1 = (bf16[4,768,576]{2,1,0:T(8,128)(2,1)}, bf16[768,896]{1,0:T(8,128)(2,1)}, f32[1,768]{1,0:T(1,128)}) custom-call(s32[1]{0:T(128)} %bitcast.2.pack_ref, bf16[1024,768]{1,0:T(8,128)(2,1)} %get-tuple-element.71.dq_ref, bf16[1024,768]{1,0:T(8,128)(2,1)} %get-tuple-element.72.dk_ref, bf16[1024,768]{1,0:T(8,128)(2,1)} %get-tuple-element.73.dv_ref, ...), custom_call_target="tpu_custom_call" | custom-call | tf_op jit(solution)/shard_map/embed_back/pallas_call | solution.py:639
  452.0 0.7 reduce-scatter.17.cloned.1.call-update
  452.8 0.7 reduce-scatter.21.cloned.1.call-update
  453.5 35.1 %reduce-scatter.11.cloned.1.call-done = bf16[96,896]{1,0:T(8,128)(2,1)} async-done(((bf16[768,896]{1,0:T(8,128)(2,1)}), bf16[96,896]{1,0:T(8,128)(2,1)}) %reduce-scatter.11.cloned.1.call-update) | async-done | bytes 172048 | tf_op jit(solution)/shard_map/reduce_scatter | solution.py:766
  488.6 42.2 %reduce-scatter.17.cloned.1.call-done = bf16[96,1000]{1,0:T(8,128)(2,1)} async-done(((bf16[768,1000]{1,0:T(8,128)(2,1)}), bf16[96,1000]{1,0:T(8,128)(2,1)}) %reduce-scatter.17.cloned.1.call-update) | async-done | bytes 192016 | tf_op jit(solution)/shard_map/reduce_scatter | solution.py:766
  533.6 1.2 slice.11
  534.9 99.0 %reduce-scatter.21.cloned.1.call-done = bf16[96,192]{1,0:T(8,128)(2,1)} async-done(((bf16[3072,192]{1,0:T(8,128)(2,1)}), bf16[96,192]{1,0:T(8,128)(2,1)}) %reduce-scatter.21.cloned.1.call-update) | async-done | bytes 36880
  633.8 0.9 copy.113
  635.4 36.4 %all-reduce.6.cloned.1.call-done = (bf16[96,896]{1,0:T(8,128)(2,1)}, bf16[96,1000]{1,0:T(8,128)(2,1)}) async-done(((bf16[96,896]{1,0:T(8,128)(2,1)}, bf16[96,1000]{1,0:T(8,128)(2,1)}), (bf16[96,896]{1,0:T(8,128)(2,1)}, bf16[96,1000]{1,0:T(8,128)(2,1)})) %all-reduce.6.cloned.1.call-update) | async-done | bytes 364048 | tf_op jit(solution)/shard_map/psum | solution.py:766
  671.8 0.9 convert_element_type.53
  672.7 1.7 multiply_reduce_fusion
  674.4 1.6 fusion
  677.3 104.1 %reduce-scatter.19.cloned.1.call-done = bf16[96,576]{1,0:T(8,128)(2,1)} async-done(((bf16[3072,576]{1,0:T(8,128)(2,1)}), bf16[96,576]{1,0:T(8,128)(2,1)}) %reduce-scatter.19.cloned.1.call-update) | async-done | bytes 110608
  781.5 1.0 copy.111
  782.5 0.7 fusion.2
  784.5 108.2 %reduce-scatter.13.cloned.1.call-done = bf16[96,768]{1,0:T(8,128)(2,1)} async-done(((bf16[3072,768]{1,0:T(8,128)(2,1)}), bf16[96,768]{1,0:T(8,128)(2,1)}) %reduce-scatter.13.cloned.1.call-update) | async-done | bytes 147472 | tf_op jit(solution)/shard_map/reduce_scatter | solution.py:761
  892.7 1.6 fusion.3
  894.9 110.2 %reduce-scatter.15.cloned.1.call-done = bf16[96,768]{1,0:T(8,128)(2,1)} async-done(((bf16[3072,768]{1,0:T(8,128)(2,1)}), bf16[96,768]{1,0:T(8,128)(2,1)}) %reduce-scatter.15.cloned.1.call-update) | async-done | bytes 147472 | tf_op jit(solution)/shard_map/reduce_scatter | solution.py:761
  1005.2 1.6 fusion.4
  1007.4 40.6 %all-reduce.2 = (f32[]{:T(128)}, f32[4,768]{1,0:T(4,128)S(1)}, f32[2,64]{1,0:T(2,128)S(1)}, f32[]{:T(128)}) all-reduce(f32[]{:T(128)S(6)} %add.187, f32[4,768]{1,0:T(4,128)S(1)} %pad_maximum_fusion.1, f32[2,64]{1,0:T(2,128)S(1)} %reduce_sum.97, f32[]{:T(128)} %bitcast.29), channel_id=1, replica_groups=mesh['dp'=8,'tensor'=4] {'tensor','dp'}, use_global_device_ids=true, to_apply=%region_15.16 | all-reduce | flops 3202 | bytes 25616 | tf_op jit(solution)/shard_map/psum | solution.py:774
  1051.7 0.9 copy.107
  1052.6 0.9 copy.108
  1053.5 0.9 copy.109
  1054.4 1.8 multiply_subtract_fusion.5
  1056.2 2.4 multiply_subtract_fusion
  1059.9 0.7 multiply_subtract_fusion.6
  1060.6 1.1 multiply_subtract_fusion.2
  1061.7 1.5 multiply_subtract_fusion.1
  (126 shorter events, 9.4 us)
Async XLA Ops:
  7.2 8.3 copy-start.1
  7.2 9.0 copy-start
  7.2 9.8 copy-start.21
  7.2 11.5 %copy-start.26 = (f32[2,64]{1,0:T(2,128)S(1)}, f32[2,64]{1,0:T(2,128)}, u32[]{:S(2)}) copy-start(f32[2,64]{1,0:T(2,128)} %param.59) | copy-start | bytes 1540
  7.2 12.2 %copy-start.34 = (s32[3,8]{1,0:T(4,128)S(1)}, s32[3,8]{1,0:T(4,128)}, u32[]{:S(2)}) copy-start(s32[3,8]{1,0:T(4,128)} %param.33) | copy-start | bytes 292
  7.3 30.9 %all-gather.7.cloned.1.call-start = ((), (), s32[]{:S(2)}) async-start(), calls=%async_computation.6 | async-start | bytes 1548288 | tf_op jit(solution)/shard_map/all_gather | solution.py:748
  10.0 92.9 %all-gather.9.cloned.1.call-start = ((), (), s32[]{:S(2)}) async-start(), calls=%async_computation.7 | async-start | bytes 4055040 | tf_op jit(solution)/shard_map/all_gather | solution.py:745
  12.0 148.0 %all-gather.11.cloned.1.call-start = ((), (), s32[]{:S(2)}) async-start(), calls=%async_computation.8 | async-start | bytes 1622016 | tf_op jit(solution)/shard_map/all_gather | solution.py:745
  13.7 212.2 %all-gather.13.cloned.1.call-start = ((), (), s32[]{:S(2)}) async-start(), calls=%async_computation.9 | async-start | bytes 4866048 | tf_op jit(solution)/shard_map/all_gather | solution.py:745
  15.4 276.3 %all-gather.15.cloned.1.call-start = ((), (), s32[]{:S(2)}) async-start(), calls=%async_computation.10 | async-start | bytes 4866048 | tf_op jit(solution)/shard_map/all_gather | solution.py:745
  16.2 309.6 %all-gather.17.cloned.1.call-start = ((), (), s32[]{:S(2)}) async-start(), calls=%async_computation.11 | async-start | bytes 1769472 | tf_op jit(solution)/shard_map/all_gather | solution.py:753
  17.0 471.6 %reduce-scatter.11.cloned.1.call-start = ((), (), s32[]{:S(2)}) async-start(), calls=%async_computation.12 | async-start | bytes 1548288 | tf_op jit(solution)/shard_map/reduce_scatter | solution.py:766
  452.0 78.8 %reduce-scatter.17.cloned.1.call-start = ((), (), s32[]{:S(2)}) async-start(), calls=%async_computation.15 | async-start | bytes 1769472 | tf_op jit(solution)/shard_map/reduce_scatter | solution.py:766
  452.7 181.1 %reduce-scatter.21.cloned.1.call-start = ((), (), s32[]{:S(2)}) async-start(), calls=%async_computation.17 | async-start | bytes 1622016
  453.4 218.3 %all-reduce.6.cloned.1.call-start = ((), (), s32[]{:S(2)}) async-start(), calls=%async_computation.18 | async-start | bytes 737280 | tf_op jit(solution)/shard_map/psum | solution.py:766
  530.7 250.7 %reduce-scatter.19.cloned.1.call-start = ((), (), s32[]{:S(2)}) async-start(), calls=%async_computation.16 | async-start | bytes 4055040
  531.5 361.2 %reduce-scatter.13.cloned.1.call-start = ((), (), s32[]{:S(2)}) async-start(), calls=%async_computation.13 | async-start | bytes 4866048 | tf_op jit(solution)/shard_map/reduce_scatter | solution.py:761
  532.1 1.0 copy-start.3
  532.1 1.1 copy-start.14
  532.1 1.3 copy-start.15
  532.1 473.1 %reduce-scatter.15.cloned.1.call-start = ((), (), s32[]{:S(2)}) async-start(), calls=%async_computation.14 | async-start | bytes 4866048 | tf_op jit(solution)/shard_map/reduce_scatter | solution.py:761
  532.1 1.4 copy-start.25
  532.2 2.7 copy-start.24
  532.2 2.7 copy-start.28
  532.2 2.7 copy-start.29
  534.9 519.5 %copy-start.9 = (f32[192,96]{1,0:T(8,128)S(1)}, f32[192,96]{1,0:T(8,128)}, u32[]{:S(2)}) copy-start(f32[192,96]{1,0:T(8,128)} %param.44) | copy-start | bytes 221188
  672.7 383.5 %copy-start.5 = (bf16[96,1000]{1,0:T(8,128)(2,1)S(1)}, bf16[96,1000]{1,0:T(8,128)(2,1)}, u32[]{:S(2)}) copy-start(bf16[96,1000]{1,0:T(8,128)(2,1)} %get-tuple-element.179) | copy-start | bytes 576004
  1048.0 3.4 copy-start.32
  1051.4 7.2 copy-start.8
  1051.4 7.2 copy-start.22
  1051.4 7.2 copy-start.23
  1051.7 8.9 copy-start.4
  1051.7 8.9 copy-start.6
  1053.4 8.2 copy-start.2
  1053.4 8.2 copy-start.7
  1053.4 8.2 copy-start.10
  1053.4 8.2 copy-start.11
  1053.4 8.2 copy-start.12
  1054.3 4.9 copy-start.27
  1054.3 4.9 copy-start.30
  1054.3 4.9 copy-start.31
  1054.3 4.9 copy-start.33
  1054.4 5.5 copy-start.18
  1054.4 5.5 copy-start.19
  1054.4 5.5 copy-start.20
  1054.4 6.2 copy-start.16
  1054.4 6.2 copy-start.17
  1054.4 7.3 copy-start.13
Sparse Core Ops, SparseCore 0:
  10.5 27.5 all-gather.6
  41.7 61.1 all-gather.8
  106.3 53.6 all-gather.10
  163.3 62.5 all-gather.12
  229.2 62.4 all-gather.14
  294.0 24.4 all-gather.16
  452.1 36.4 reduce-scatter.10
  492.2 38.4 reduce-scatter.16
  536.8 96.9 reduce-scatter.20
  636.2 35.4 all-reduce.5
  677.2 104.2 reduce-scatter.18
  786.8 105.8 reduce-scatter.12
  899.1 106.0 reduce-scatter.14

commit v2 on v1

--- a/solution.py
+++ b/solution.py
@@ -695,6 +695,477 @@
     return (d_pp, d_in, d_out, d_up, d_dn, d_cls), d_vectors, d_gains, loss[0, 0]
 
 
+MESH = pl.DeviceIdType.MESH
+
+
+class Seat:
+    def __init__(self):
+        self.me = lax.axis_index("dp")
+        self.z = lax.axis_index("tensor")
+        self.c = lax.rem(self.me, 2)
+        self.x = lax.rem(lax.div(self.me, 2), 2)
+        self.y = lax.div(self.me, 4)
+        self.core = self.me + 1 - 2 * self.c
+        self.xn = self.me + 2 - 4 * self.x
+        self.yn = self.me + 4 - 8 * self.y
+        self.diag = self.xn + 4 - 8 * self.y
+
+
+def link(src, dst, sems, at, device):
+    return pltpu.make_async_remote_copy(
+        src_ref=src,
+        dst_ref=dst,
+        send_sem=sems[0].at[at],
+        recv_sem=sems[1].at[at],
+        device_id=device,
+        device_id_type=MESH,
+    )
+
+
+def greet(seat, depth):
+    barrier = pltpu.get_barrier_semaphore()
+    for near in (seat.core, seat.xn, seat.yn):
+        pl.semaphore_signal(barrier, inc=1, device_id={"dp": near}, device_id_type=MESH)
+    for ahead in range(1, depth):
+        pl.semaphore_signal(
+            barrier, inc=1, device_id={"tensor": lax.rem(seat.z + ahead, depth)}, device_id_type=MESH
+        )
+    pl.semaphore_wait(barrier, 2 + depth)
+
+
+def gather_kernel(*refs, count, split):
+    shards, outs = refs[:count], refs[count : 2 * count]
+    own_sem, send_sem, recv_sem = refs[2 * count :]
+    sems = (send_sem, recv_sem)
+    seat = Seat()
+    depth = 4
+    share = shards[0].shape[0]
+    half = share // 2
+    greet(seat, depth)
+
+    def rows(owner):
+        return pl.ds(pl.multiple_of(owner * share, share), share)
+
+    def column(k, owner):
+        return outs[k].at[:, rows(owner), :] if split[k] else outs[k].at[rows(owner), :]
+
+    def halves(k, owner, which):
+        if split[k]:
+            return outs[k].at[pl.ds(2 * which, 2), rows(owner), :]
+        return outs[k].at[pl.ds(pl.multiple_of(owner * share + which * half, half), half), :]
+
+    def block(k, level):
+        return outs[k].at[level, rows(seat.me), :]
+
+    def keep(k):
+        mine = block(k, seat.z) if split[k] else column(k, seat.me)
+        return pltpu.make_async_copy(shards[k], mine, own_sem.at[k])
+
+    def along(k, hop, way):
+        level = seat.z - way * hop
+        source = shards[k] if hop == 0 else block(k, level)
+        at = (k, hop + (0 if way > 0 else 3))
+        return link(source, block(k, level), sems, at, {"tensor": seat.z + way})
+
+    def arrives(k, hop, way):
+        level = seat.z - way * (hop + 1)
+        at = (k, hop + (0 if way > 0 else 3))
+        return link(block(k, level), block(k, level), sems, at, {"tensor": seat.z - way})
+
+    def sends(hop, way):
+        level, to = seat.z - way * hop, seat.z + way
+        return (level >= 0) & (level < depth) & (to >= 0) & (to < depth)
+
+    def gets(hop, way):
+        level = seat.z - way * (hop + 1)
+        return (level >= 0) & (level < depth)
+
+    def start_z(k):
+        keep(k).start()
+        if split[k]:
+            for way in (1, -1):
+
+                @pl.when(sends(0, way))
+                def _():
+                    along(k, 0, way).start()
+
+    def relay_z(k):
+        if split[k]:
+            for hop in range(depth - 1):
+                for way in (1, -1):
+
+                    @pl.when(gets(hop, way))
+                    def _():
+                        arrives(k, hop, way).wait_recv()
+
+                    if hop + 1 < depth - 1:
+
+                        @pl.when(sends(hop + 1, way))
+                        def _():
+                            along(k, hop + 1, way).start()
+
+    def own_x(k):
+        return link(column(k, seat.me), column(k, seat.me), sems, (k, 6), {"dp": seat.xn})
+
+    def own_y(k):
+        return link(column(k, seat.me), column(k, seat.me), sems, (k, 7), {"dp": seat.yn})
+
+    def pass_x(k):
+        return link(halves(k, seat.yn, 1), halves(k, seat.yn, 1), sems, (k, 8), {"dp": seat.xn})
+
+    def pass_y(k):
+        return link(halves(k, seat.xn, 0), halves(k, seat.xn, 0), sems, (k, 9), {"dp": seat.yn})
+
+    def over(k, which):
+        owner = (seat.me, seat.xn, seat.yn, seat.diag)[which]
+        return link(column(k, owner), column(k, owner), sems, (k, 10 + which), {"dp": seat.core})
+
+    def wait_column(k, at, region, device):
+        link(region, region, sems, (k, at), device).wait_recv()
+
+    def start_plane(k):
+        keep(k).wait()
+        own_x(k).start()
+        own_y(k).start()
+        over(k, 0).start()
+
+    def relay_plane(k):
+        wait_column(k, 6, column(k, seat.xn), {"dp": seat.xn})
+        pass_y(k).start()
+        over(k, 1).start()
+        wait_column(k, 7, column(k, seat.yn), {"dp": seat.yn})
+        pass_x(k).start()
+        over(k, 2).start()
+
+    def finish_plane(k):
+        wait_column(k, 8, halves(k, seat.diag, 1), {"dp": seat.xn})
+        wait_column(k, 9, halves(k, seat.diag, 0), {"dp": seat.yn})
+        over(k, 3).start()
+
+    def drain(k):
+        for which, shift in ((0, 0), (1, 1), (2, 2), (3, 3)):
+            owner = (seat.me, seat.xn, seat.yn, seat.diag)[which] + 1 - 2 * seat.c
+            wait_column(k, 10 + which, column(k, owner), {"dp": seat.core})
+        if split[k]:
+            for hop in range(depth - 1):
+                for way in (1, -1):
+
+                    @pl.when(sends(hop, way))
+                    def _():
+                        along(k, hop, way).wait_send()
+
+        for copy in (own_x(k), own_y(k), pass_x(k), pass_y(k)):
+            copy.wait_send()
+        for which in range(4):
+            over(k, which).wait_send()
+
+    for k in range(count):
+        start_z(k)
+    for turn in range(count + 2):
+        if turn < count:
+            relay_z(turn)
+            start_plane(turn)
+        if 0 <= turn - 1 < count:
+            relay_plane(turn - 1)
+        if 0 <= turn - 2 < count:
+            finish_plane(turn - 2)
+    for k in range(count):
+        drain(k)
+
+
+def gather_call(shards, split, depth, width, collective_id):
+    count = len(shards)
+    shapes = [
+        jax.ShapeDtypeStruct(((depth, width) if apart else (width,)) + entry.shape[1:], entry.dtype)
+        for entry, apart in zip(shards, split)
+    ]
+    return pl.pallas_call(
+        functools.partial(gather_kernel, count=count, split=split),
+        out_shape=shapes,
+        in_specs=[pl.BlockSpec(memory_space=pl.ANY)] * count,
+        out_specs=[pl.BlockSpec(memory_space=pl.ANY)] * count,
+        scratch_shapes=[
+            pltpu.SemaphoreType.DMA((count,)),
+            pltpu.SemaphoreType.DMA((count, 14)),
+            pltpu.SemaphoreType.DMA((count, 14)),
+        ],
+        compiler_params=pltpu.CompilerParams(
+            collective_id=collective_id, has_side_effects=True, vmem_limit_bytes=VMEM_BYTES
+        ),
+        name="gather_weights",
+    )(*shards)
+
+
+def scatter_kernel(*refs, count, split):
+    grads, small_ref = refs[:count], refs[count]
+    outs, small_out, square_out = refs[count + 1 : 2 * count + 1], refs[2 * count + 1], refs[2 * count + 2]
+    rest = refs[2 * count + 3 :]
+    own, core_in, one_x, one_y, two_x, two_y, up_in, down_in, result = (
+        rest[k * count : (k + 1) * count] for k in range(9)
+    )
+    tiny, tiny_in, own_sem, send_sem, recv_sem, tiny_send, tiny_recv, out_sem = rest[9 * count :]
+    sems = (send_sem, recv_sem)
+    seat = Seat()
+    depth = 4
+    x, y, z, c = seat.x, seat.y, seat.z, seat.c
+    dp = lambda near: {"dp": near}
+
+    def load(k):
+        source = grads[k].at[:, :, :, c] if split[k] else grads[k].at[:, :, c]
+        return pltpu.make_async_copy(source, own[k], own_sem.at[k])
+
+    def to_core(k):
+        source = grads[k].at[:, :, :, 1 - c] if split[k] else grads[k].at[:, :, 1 - c]
+        return link(source, core_in[k], sems, (k, 0), dp(seat.core))
+
+    def first_x(k):
+        half = own[k].shape[-2] // 2
+        source = own[k].at[0:2, :, 1 - x] if split[k] else own[k].at[:, 1 - x, 0:half]
+        return link(source, one_x[k], sems, (k, 1), dp(seat.xn))
+
+    def first_y(k):
+        half = own[k].shape[-2] // 2
+        source = own[k].at[2:4, 1 - y] if split[k] else own[k].at[1 - y, :, half : 2 * half]
+        return link(source, one_y[k], sems, (k, 2), dp(seat.yn))
+
+    def second_y(k):
+        half = own[k].shape[-2] // 2
+        source = own[k].at[0:2, 1 - y, x] if split[k] else own[k].at[1 - y, x, 0:half]
+        return link(source, two_y[k], sems, (k, 3), dp(seat.yn))
+
+    def second_x(k):
+        half = own[k].shape[-2] // 2
+        source = own[k].at[2:4, y, 1 - x] if split[k] else own[k].at[y, 1 - x, half : 2 * half]
+        return link(source, two_x[k], sems, (k, 4), dp(seat.xn))
+
+    def along(k, level, way):
+        buffer = up_in if way > 0 else down_in
+        at = (k, 5 + level if way > 0 else 9 + level)
+        return link(own[k].at[level, y, x], buffer[k].at[level], sems, at, {"tensor": z + way})
+
+    def whole_z(k, ahead):
+        to = lax.rem(z + ahead, depth)
+        return link(own[k].at[y, x], up_in[k].at[z], sems, (k, 5 + ahead), {"tensor": to})
+
+    def whole_from(k, ahead):
+        source = lax.rem(z - ahead + depth, depth)
+        return link(own[k].at[y, x], up_in[k].at[source], sems, (k, 5 + ahead), {"tensor": source})
+
+    def stage_one(k):
+        load(k).wait()
+        to_core(k).wait_recv()
+        lead = own[k].shape[:-2]
+        blocks = 1
+        for size in lead:
+            blocks *= size
+
+        def add(b, carry):
+            at, left = [], b
+            for size in lead[::-1]:
+                at.append(lax.rem(left, size))
+                left = lax.div(left, size)
+            at = tuple(at[::-1])
+            own[k][at] = own[k][at] + core_in[k][at]
+            return carry
+
+        lax.fori_loop(0, blocks, add, 0)
+        first_x(k).start()
+        first_y(k).start()
+
+    def stage_two(k):
+        half = own[k].shape[-2] // 2
+        first_x(k).wait_recv()
+        for a in range(2):
+            for b in range(2 if split[k] else 1):
+                if split[k]:
+                    own[k][a, b, x] = own[k][a, b, x] + one_x[k][a, b]
+                else:
+                    own[k][a, x, 0:half] = own[k][a, x, 0:half] + one_x[k][a]
+        second_y(k).start()
+        first_y(k).wait_recv()
+        for a in range(2):
+            for b in range(2 if split[k] else 1):
+                if split[k]:
+                    own[k][2 + a, y, b] = own[k][2 + a, y, b] + one_y[k][a, b]
+                else:
+                    own[k][y, a, half : 2 * half] = own[k][y, a, half : 2 * half] + one_y[k][a]
+        second_x(k).start()
+
+    def stage_three(k):
+        half = own[k].shape[-2] // 2
+        second_y(k).wait_recv()
+        second_x(k).wait_recv()
+        if split[k]:
+            for a in range(2):
+                own[k][a, y, x] = own[k][a, y, x] + two_y[k][a]
+                own[k][2 + a, y, x] = own[k][2 + a, y, x] + two_x[k][a]
+            for way in (1, -1):
+
+                @pl.when(z == (0 if way > 0 else depth - 1))
+                def _():
+                    for level in range(depth):
+                        far = depth - 1 - level if way > 0 else level
+                        if far != (0 if way > 0 else depth - 1):
+                            along(k, far, way).start()
+        else:
+            own[k][y, x, 0:half] = own[k][y, x, 0:half] + two_y[k][...]
+            own[k][y, x, half : 2 * half] = own[k][y, x, half : 2 * half] + two_x[k][...]
+            for ahead in range(1, depth):
+                whole_z(k, ahead).start()
+
+    def stage_four(k):
+        if split[k]:
+            for level in range(depth):
+                far = depth - 1 - level
+
+                @pl.when((z > 0) & (z < far))
+                def _():
+                    along(k, far, 1).wait_recv()
+                    own[k][far, y, x] = own[k][far, y, x] + up_in[k][far]
+                    along(k, far, 1).start()
+
+                @pl.when((z < depth - 1) & (z > level))
+                def _():
+                    along(k, level, -1).wait_recv()
+                    own[k][level, y, x] = own[k][level, y, x] + down_in[k][level]
+                    along(k, level, -1).start()
+
+            result[k][...] = own[k][z, y, x].astype(F32)
+
+            @pl.when(z > 0)
+            def _():
+                along(k, z, 1).wait_recv()
+                result[k][...] += up_in[k][z].astype(F32)
+
+            @pl.when(z < depth - 1)
+            def _():
+                along(k, z, -1).wait_recv()
+                result[k][...] += down_in[k][z].astype(F32)
+
+            factor = 1.0
+        else:
+            for ahead in range(1, depth):
+                whole_from(k, ahead).wait_recv()
+            up_in[k][z] = own[k][y, x]
+            total = up_in[k][0].astype(F32)
+            for level in range(1, depth):
+                total += up_in[k][level].astype(F32)
+            result[k][...] = total
+            factor = jnp.where(z == 0, 1.0, 0.0)
+        pltpu.make_async_copy(result[k], outs[k], out_sem.at[k]).start()
+        values = result[k][...]
+        return jnp.sum(jnp.sum(values * values, axis=0, keepdims=True), axis=1, keepdims=True) * factor
+
+    def drain(k):
+        pltpu.make_async_copy(result[k], outs[k], out_sem.at[k]).wait()
+        for copy in (to_core(k), first_x(k), first_y(k), second_x(k), second_y(k)):
+            copy.wait_send()
+        if split[k]:
+            for level in range(depth):
+
+                @pl.when(z < level)
+                def _():
+                    along(k, level, 1).wait_send()
+
+                @pl.when(z > level)
+                def _():
+                    along(k, level, -1).wait_send()
+
+        else:
+            for ahead in range(1, depth):
+                whole_z(k, ahead).wait_send()
+
+    def tiny_sum(which, first):
+        view = tiny[which]
+        came = tiny_in[which]
+        tsems = (tiny_send, tiny_recv)
+        for hop, near in enumerate((seat.core, seat.xn, seat.yn)):
+            copy = link(view.at[0], came.at[hop], tsems, (which, hop), dp(near))
+            copy.start()
+            copy.wait_recv()
+            copy.wait_send()
+            view[0] = view[0] + came[hop]
+        copies = []
+        for ahead in range(1, depth):
+            to = lax.rem(z + ahead, depth)
+            copies.append(link(view.at[0], came.at[3 + z], tsems, (which, 2 + ahead), {"tensor": to}))
+            copies[-1].start()
+        for ahead in range(1, depth):
+            source = lax.rem(z - ahead + depth, depth)
+            link(view.at[0], came.at[3 + source], tsems, (which, 2 + ahead), {"tensor": source}).wait_recv()
+        for copy in copies:
+            copy.wait_send()
+        came[3 + z] = view[0]
+        total = came[3]
+        for level in range(1, depth):
+            total = total + came[3 + level]
+        view[0] = total
+
+    for k in range(count):
+        load(k).start()
+    greet(seat, depth)
+    for k in range(count):
+        to_core(k).start()
+    squares = jnp.zeros((1, 1), F32)
+    for turn in range(count + 3):
+        if turn < count:
+            stage_one(turn)
+        if 0 <= turn - 1 < count:
+            stage_two(turn - 1)
+        if 0 <= turn - 2 < count:
+            stage_three(turn - 2)
+        if turn == count:
+            tiny[0][0] = small_ref[...]
+            tiny_sum(0, True)
+            small_out[...] = tiny[0][0]
+        if 0 <= turn - 3 < count:
+            squares = squares + stage_four(turn - 3)
+    tiny[1][0] = jnp.broadcast_to(squares, tiny[1].shape[1:])
+    tiny_sum(1, False)
+    square_out[...] = tiny[1][0]
+    for k in range(count):
+        drain(k)
+
+
+def scatter_call(grads, small, split, collective_id):
+    count = len(grads)
+    depth = 4
+    tails = [entry.shape[-2:] for entry in grads]
+    own, core_in, one, two, up = [], [], [], [], []
+    for entry, apart, (share, cols) in zip(grads, split, tails):
+        lead = (depth, 2, 2) if apart else (2, 2)
+        own.append(pltpu.VMEM(lead + (share, cols), LOW))
+        core_in.append(pltpu.VMEM(lead + (share, cols), LOW))
+        one.append(pltpu.VMEM((2, 2, share, cols) if apart else (2, share // 2, cols), LOW))
+        two.append(pltpu.VMEM((2, share, cols) if apart else (share // 2, cols), LOW))
+        up.append(pltpu.VMEM((depth, share, cols), LOW))
+    results = [pltpu.VMEM(tail, F32) for tail in tails]
+    anywhere = pl.BlockSpec(memory_space=pl.ANY)
+    inside = pl.BlockSpec(memory_space=pltpu.VMEM)
+    return pl.pallas_call(
+        functools.partial(scatter_kernel, count=count, split=split),
+        out_shape=[jax.ShapeDtypeStruct(tail, F32) for tail in tails]
+        + [jax.ShapeDtypeStruct(small.shape, F32), jax.ShapeDtypeStruct((8, 128), F32)],
+        in_specs=[anywhere] * count + [inside],
+        out_specs=[anywhere] * count + [inside, inside],
+        scratch_shapes=own + core_in + one + one + two + two + up + up + results
+        + [
+            [pltpu.VMEM((1,) + small.shape, F32), pltpu.VMEM((1, 8, 128), F32)],
+            [pltpu.VMEM((7,) + small.shape, F32), pltpu.VMEM((7, 8, 128), F32)],
+            pltpu.SemaphoreType.DMA((count,)),
+            pltpu.SemaphoreType.DMA((count, 13)),
+            pltpu.SemaphoreType.DMA((count, 13)),
+            pltpu.SemaphoreType.DMA((2, 6)),
+            pltpu.SemaphoreType.DMA((2, 6)),
+            pltpu.SemaphoreType.DMA((count,)),
+        ],
+        compiler_params=pltpu.CompilerParams(
+            collective_id=collective_id, has_side_effects=True, vmem_limit_bytes=VMEM_BYTES
+        ),
+        name="scatter_grads",
+    )(*grads, small)
+
+
 def adam(master, first_moment, second_moment, gradient, clip_scale, rate, decay_rate):
     gradient = gradient * clip_scale
     first_new = BETA_ONE * first_moment + (1 - BETA_ONE) * gradient
@@ -740,38 +1211,60 @@
         classify.astype(LOW),
     )
     both = ("tensor", "dp")
-
-    def gather(shard):
-        return lax.all_gather(shard, both, axis=0, tiled=True).reshape(members, width, -1)
-
-    weights = (
-        lax.all_gather(shards[0], "dp", axis=0, tiled=True),
-        gather(shards[1]),
-        gather(shards[2]),
-        gather(shards[3]),
-        gather(shards[4]),
-        lax.all_gather(shards[5], "dp", axis=0, tiled=True),
-    )
+    close = lax.axis_size("dp") == 8 and members == 4
+    if close:
+        weights = gather_call(shards, (False, True, True, True, True, False), members, width, 0)
+    else:
+
+        def gather(shard):
+            return lax.all_gather(shard, both, axis=0, tiled=True).reshape(members, width, -1)
+
+        weights = (
+            lax.all_gather(shards[0], "dp", axis=0, tiled=True),
+            gather(shards[1]),
+            gather(shards[2]),
+            gather(shards[3]),
+            gather(shards[4]),
+            lax.all_gather(shards[5], "dp", axis=0, tiled=True),
+        )
     grads, grad_vectors, grad_gains, loss_local = pack_step(
         pack, valid, pixels, coords, lengths, labels, weights, vectors, head_gains, image_count
     )
-    grad_vectors, grad_gains, loss_total = lax.psum((grad_vectors, grad_gains, loss_local), both)
-
-    def scatter(grad):
-        return lax.psum_scatter(
-            grad.reshape(members * width, -1), both, scatter_dimension=0, tiled=True
-        ).astype(F32)
-
-    def scatter_whole(grad):
-        return lax.psum(lax.psum_scatter(grad, "dp", scatter_dimension=0, tiled=True), "tensor").astype(F32)
-
-    share_pp = scatter_whole(grads[0])
-    share_in, share_out, share_up, share_dn = (scatter(entry) for entry in grads[1:5])
-    share_cls = scatter_whole(grads[5])
-    leader = (seat == 0).astype(F32)
-    split_squares = squared(share_in) + squared(share_out) + squared(share_up) + squared(share_dn)
-    whole_squares = squared(share_pp) + squared(share_cls)
-    squares = lax.psum(split_squares + leader * whole_squares, both)
+    if close:
+        d_pp, d_in, d_out, d_up, d_dn, d_cls = grads
+        small = jnp.zeros((16, width), F32)
+        small = small.at[:4].set(grad_vectors)
+        small = small.at[4, : grad_gains.size].set(grad_gains.reshape(-1))
+        small = small.at[5].set(loss_local)
+        cut = lambda entry: entry.reshape(entry.shape[:-2] + (2, 2, 2, share) + entry.shape[-1:])
+        share_dn, share_up, share_out, share_cls, share_in, share_pp, small, squares = scatter_call(
+            [cut(entry) for entry in (d_dn, d_up, d_out, d_cls, d_in, d_pp)],
+            small,
+            (True, True, True, False, True, False),
+            1,
+        )
+        grad_vectors = small[:4]
+        grad_gains = small[4, : head_gains.size].reshape(head_gains.shape)
+        loss_total = small[5, 0]
+        squares = squares[0, 0]
+    else:
+        grad_vectors, grad_gains, loss_total = lax.psum((grad_vectors, grad_gains, loss_local), both)
+
+        def scatter(grad):
+            return lax.psum_scatter(
+                grad.reshape(members * width, -1), both, scatter_dimension=0, tiled=True
+            ).astype(F32)
+
+        def scatter_whole(grad):
+            part = lax.psum_scatter(grad, "dp", scatter_dimension=0, tiled=True)
+            return lax.psum(part, "tensor").astype(F32)
+
+        share_pp = scatter_whole(grads[0])
+        share_in, share_out, share_up, share_dn = (scatter(entry) for entry in grads[1:5])
+        share_cls = scatter_whole(grads[5])
+        leader = (seat == 0).astype(F32)
+        split_squares = squared(share_in) + squared(share_out) + squared(share_up) + squared(share_dn)
+        squares = lax.psum(split_squares + leader * (squared(share_pp) + squared(share_cls)), both)
     grad_norm = jnp.sqrt(squares + squared(grad_vectors) + squared(grad_gains))
     clip_scale = CLIP / jnp.maximum(grad_norm, CLIP)
     pixel_width = patch_table.shape[0]

time: 1080 us -> 503 us (0.47)
  waiting for transfers between devices: 772 us -> 0 us
  Pallas kernels: 198 us -> 449 us
  blocking collectives: 40.6 us -> 0 us
  between operations: 21.7 us -> 4.59 us
    reduce_scatter x4 -> x0, waiting for transfers between devices: 296 us -> none  [the longest x2 218 us: scatter(): lax.psum_scatter(grad.reshape(members * width, -1), both, scatter_dimensi...]
    pallas_call x0 -> x2, Pallas kernels: none -> 250 us  [the longest x1 156 us: scatter_call(): pl.pallas_call(functools.partial(scatter_kernel, count=count, split=split...]
    all_gather x6 -> x0, waiting for transfers between devices: 234 us -> none  [the longest x4 216 us: gather(): lax.all_gather(shard, both, axis=0, tiled=True).reshape(members, width, -1)]
    unnamed x15 -> x0, waiting for transfers between devices: 206 us -> none
    psum x1 -> x0, blocking collectives: 40.6 us -> none  [per_device(): squares = lax.psum(split_squares + leader * whole_squares, both)]
    psum x1 -> x0, waiting for transfers between devices: 36.4 us -> none  [scatter_whole(): lax.psum(lax.psum_scatter(grad, 'dp', scatter_dimension=0, tiled=True), '...]
  transfers between devices with their start and end apart: 13 -> 0, of which waited for: 12 -> 0; matrix products, arithmetic and copies ran while one was open for 2% -> 0% of each run, Pallas kernels for 7% -> 0%
where the time goes in v2:
time: 503 us; the launch traced here: 494 us
  Pallas kernels  449 us (89%)
  other arithmetic  23.7 us (5%)
  local copies, waits for them, and re-layouts  16.6 us (3%)
    pallas_call x1, Pallas kernels, scatter_call(): pl.pallas_call(functools.partial(scatter_kernel, count=count, split=split...  156 us
    pallas_call x1, Pallas kernels, gather_call(): pl.pallas_call(functools.partial(gather_kernel, count=count, split=split)...  94.7 us
    pallas_call x1, Pallas kernels, attend_back_call(): pl.pallas_call(attend_back_kernel, grid=(pairs,), in_specs=[pair] * 6 + [...  47.5 us
    pallas_call x1, Pallas kernels, mlp_back_call(): pl.pallas_call(mlp_back_kernel, grid=(hidden // chunk,), in_specs=[whole(...  44 us
    pallas_call x1, Pallas kernels, mlp_call(): pl.pallas_call(mlp_kernel, grid=(hidden // chunk,), in_specs=[whole(atten...  34.2 us
    pallas_call x1, Pallas kernels, embed_back_call(): pl.pallas_call(embed_back_kernel, grid_spec=pltpu.PrefetchScalarGridSpec(...  23.8 us
    pallas_call x1, Pallas kernels, attend_call(): pl.pallas_call(attend_kernel, grid=(width // 128,), in_specs=[pair, pair,...  23.6 us
    pallas_call x1, Pallas kernels, embed_call(): pl.pallas_call(embed_kernel, grid_spec=pltpu.PrefetchScalarGridSpec(num_s...  14.2 us

profile of v2, /device:TPU:0, one launch (start us, length us, event | category | flops | bytes accessed | tf_op | source)
XLA Modules:
  0.0 493.6 jit_solution(15602169930484740582)
XLA Ops:
  0.7 0.7 fusion.9
  1.4 0.2 reduce-window.9
  1.6 0.7 bitcast_subtract_fusion
  2.5 0.6 pad_add_fusion.bound_ref
  3.1 1.0 copy.98
  4.0 0.6 convert_bitcast_fusion.2.refs_2_
  4.7 1.0 convert_element_type.23
  5.7 0.2 copy.97
  5.8 0.8 copy.99.refs_1_
  6.6 1.0 convert_bitcast_fusion.1
  7.6 0.8 convert.11
  8.5 0.7 pad_maximum_fusion.refs_0_
  9.2 1.7 convert_element_type.30.refs_5_
  10.9 1.6 convert_bitcast_fusion.refs_4_
  12.6 0.7 convert_element_type.27.refs_3_
  13.3 94.7 %gather_weights.1 = (bf16[768,896]{1,0:T(8,128)(2,1)}, bf16[4,768,576]{2,1,0:T(8,128)(2,1)}, bf16[4,768,192]{2,1,0:T(8,128)(2,1)}, bf16[4,768,768]{2,1,0:T(8,128...) custom-call(bf16[96,896]{1,0:T(8,128)(2,1)} %pad_maximum_fusion.refs_0_, bf16[96,576]{1,0:T(8,128)(2,1)} %copy.99.refs_1_, ...), custom_call_target="tpu_custom_call" | custom-call | tf_op jit(solution)/shard_map/gather_weights/pallas_call | solution.py:882
  108.0 1.7 copy.95
  109.7 14.2 %embed.1 = (f32[1024,768]{1,0:T(8,128)}, bf16[1024,768]{1,0:T(8,128)(2,1)}, f32[1024,768]{1,0:T(8,128)}, f32[1024,768]{1,0:T(8,128)}, bf16[1024,768]{1,0:T(8,128)(2,1)}) custom-call(s32[1]{0:T(128)} %bitcast.pack_ref, bf16[3072,768]{1,0:T(8,128)(2,1)} %pix_ref.3, s32[3072,2]{1,0:T(8,128)} %bitcast.47, bf16[768,896]{1,0:T(8,128)(2,1)} %get-tuple-element.108.wp_ref, ...), custom_call_target="tpu_custom_call" | custom-call | tf_op jit(solution)/shard_map/embed/pallas_call | solution.py:134
  123.9 0.6 tile.9.gain_ref
  124.6 23.6 %attend.1 = (bf16[1024,768]{1,0:T(8,128)(2,1)}, f32[1024,768]{1,0:T(8,128)}) custom-call(f32[1024,768]{1,0:T(8,128)} %get-tuple-element.110.q_ref, f32[1024,768]{1,0:T(8,128)} %get-tuple-element.111.k_ref, bf16[1024,768]{1,0:T(8,128)(2,1)} %get-tuple-element.112.v_ref, f32[2,128]{1,0:T(2,128)} %tile.9.gain_ref, s32[2,128]{1,0:T(2,128)} %pad_add_fusion.bound_ref), custom_call_target="tpu_custom_call" | custom-call | tf_op jit(solution)/shard_map/attend/pallas_call | solution.py:208
  148.2 34.2 %mlp.1 = (f32[1024,768]{1,0:T(8,128)}, bf16[1024,768]{1,0:T(8,128)(2,1)}, bf16[1024,3072]{1,0:T(8,128)(2,1)}, bf16[1024,3072]{1,0:T(8,128)(2,1)}, f32[1024,768]{1,0:T(8,128)}) custom-call(bf16[1024,768]{1,0:T(8,128)(2,1)} %get-tuple-element.113.o_ref, f32[1024,768]{1,0:T(8,128)} %get-tuple-element.114.emb_ref, ...), custom_call_target="tpu_custom_call" | custom-call | tf_op jit(solution)/shard_map/mlp/pallas_call | solution.py:365
  182.5 11.1 %pool.1 = (f32[1024,768]{1,0:T(8,128)}, bf16[768,1000]{1,0:T(8,128)(2,1)}, f32[8,128]{1,0:T(8,128)}, f32[2,768]{1,0:T(2,128)}) custom-call(s32[1]{0:T(128)} %bitcast.pack_ref, f32[1024,768]{1,0:T(8,128)} %get-tuple-element.118.x2_ref, s32[24,1000]{1,0:T(8,128)} %label_ref.1, bf16[768,1000]{1,0:T(8,128)(2,1)} %get-tuple-element.119.wcls_ref, ...), custom_call_target="tpu_custom_call" | custom-call | tf_op jit(solution)/shard_map/pool/pallas_call | solution.py:461
  193.6 44.0 %mlp_back.1 = (bf16[4,768,768]{2,1,0:T(8,128)(2,1)}, bf16[4,768,768]{2,1,0:T(8,128)(2,1)}, bf16[4,768,192]{2,1,0:T(8,128)(2,1)}, bf16[1024,768]{1,0:T(8,128)(2,1...) custom-call(f32[1024,768]{1,0:T(8,128)} %get-tuple-element.120.dx2_ref, bf16[1024,3072]{1,0:T(8,128)(2,1)} %get-tuple-element.121.act_ref, ...), custom_call_target="tpu_custom_call" | custom-call | tf_op jit(solution)/shard_map/mlp_back/pallas_call | solution.py:551
  237.5 47.5 %attend_back.1 = (bf16[1024,768]{1,0:T(8,128)(2,1)}, bf16[1024,768]{1,0:T(8,128)(2,1)}, bf16[1024,768]{1,0:T(8,128)(2,1)}, f32[6,2,128]{2,1,0:T(2,128)}) custom-call(f32[1024,768]{1,0:T(8,128)} %get-tuple-element.110.q_ref, f32[1024,768]{1,0:T(8,128)} %get-tuple-element.111.k_ref, bf16[1024,768]{1,0:T(8,128)(2,1)} %get-tuple-element.112.v_ref, ...), custom_call_target="tpu_custom_call" | custom-call | tf_op jit(solution)/shard_map/attend_back/pallas_call | solution.py:306
  285.1 23.8 %embed_back.1 = (bf16[4,768,576]{2,1,0:T(8,128)(2,1)}, bf16[768,896]{1,0:T(8,128)(2,1)}, f32[1,768]{1,0:T(1,128)}) custom-call(s32[1]{0:T(128)} %bitcast.pack_ref, bf16[1024,768]{1,0:T(8,128)(2,1)} %get-tuple-element.131.dq_ref, bf16[1024,768]{1,0:T(8,128)(2,1)} %get-tuple-element.132.dk_ref, bf16[1024,768]{1,0:T(8,128)(2,1)} %get-tuple-element.133.dv_ref, ...), custom_call_target="tpu_custom_call" | custom-call | tf_op jit(solution)/shard_map/embed_back/pallas_call | solution.py:639
  308.9 0.7 select_maximum_fusion
  310.0 1.2 slice.71
  311.2 0.6 broadcast.148
  311.9 0.6 copy-done.16
  312.6 155.6 %scatter_grads.1 = (f32[96,768]{1,0:T(8,128)}, f32[96,768]{1,0:T(8,128)}, f32[96,192]{1,0:T(8,128)}, f32[96,1000]{1,0:T(8,128)}, f32[96,576]{1,0:T(8,128)}, /*in...) custom-call(bf16[4,2,2,2,96,768]{5,4,3,2,1,0:T(8,128)(2,1)} %bitcast.49, ...), custom_call_target="tpu_custom_call" | custom-call | tf_op jit(solution)/shard_map/scatter_grads/pallas_call | solution.py:1145
  468.2 1.2 slice.73
  469.5 1.3 multiply_reduce_fusion
  472.1 1.3 multiply_reduce_fusion.2
  474.1 0.7 multiply_reduce_fusion.1
  474.9 0.6 add_subtract_fusion.1
  475.5 1.4 add_subtract_fusion
  476.9 2.3 multiply_subtract_fusion
  479.2 2.1 multiply_subtract_fusion.2
  481.6 0.7 copy.113
  482.4 0.7 copy.114
  483.1 0.7 copy.115
  484.6 0.2 multiply_subtract_fusion.3
  484.8 0.9 copy.110
  485.7 0.9 copy.111
  486.5 0.9 copy.112
  487.6 0.7 multiply_subtract_fusion.6
  488.3 2.7 multiply_subtract_fusion.1
  491.0 1.2 slice.77
  (86 shorter events, 2.0 us)
Async XLA Ops:
  0.7 11.9 %copy-start.1 = (f32[96,768]{1,0:T(8,128)S(1)}, f32[96,768]{1,0:T(8,128)}, u32[]{:S(2)}) copy-start(f32[96,768]{1,0:T(8,128)} %param.53) | copy-start | bytes 884740
  0.7 107.3 %copy-start.22 = (s32[2,3072]{1,0:T(2,128)S(1)}, s32[2,3072]{1,0:T(2,128)}, u32[]{:S(2)}) copy-start(s32[2,3072]{1,0:T(2,128)} %param.38) | copy-start | bytes 73732
  109.7 14.2 %copy-start.27 = (f32[2,64]{1,0:T(2,128)S(1)}, f32[2,64]{1,0:T(2,128)}, u32[]{:S(2)}) copy-start(f32[2,64]{1,0:T(2,128)} %param.65) | copy-start | bytes 1540
  285.1 23.8 %copy-start.26 = (f32[2,768]{1,0:T(2,128)S(1)}, f32[2,768]{1,0:T(2,128)}, u32[]{:S(2)}) copy-start(f32[2,768]{1,0:T(2,128)} %get-tuple-element.140) | copy-start | bytes 18436
  285.1 23.8 %copy-start.28 = (f32[1,768]{1,0:T(1,128)S(1)}, f32[1,768]{1,0:T(1,128)}, u32[]{:S(2)}) copy-start(f32[1,768]{1,0:T(1,128)} %get-tuple-element.139) | copy-start | bytes 9220
  285.1 24.5 %copy-start.25 = (f32[6,2,128]{2,1,0:T(2,128)S(1)}, f32[6,2,128]{2,1,0:T(2,128)}, u32[]{:S(2)}) copy-start(f32[6,2,128]{2,1,0:T(2,128)} %get-tuple-element.141) | copy-start | bytes 18436
  311.9 0.6 copy-start.16
  312.5 162.4 %copy-start.29 = (f32[2,64]{1,0:T(2,128)S(1)}, f32[2,64]{1,0:T(2,128)}, u32[]{:S(2)}) copy-start(f32[2,64]{1,0:T(2,128)} %param.66) | copy-start | bytes 1540
  312.5 162.4 %copy-start.30 = (f32[2,64]{1,0:T(2,128)S(1)}, f32[2,64]{1,0:T(2,128)}, u32[]{:S(2)}) copy-start(f32[2,64]{1,0:T(2,128)} %param.67) | copy-start | bytes 1540
  312.5 163.0 %copy-start.5 = (f32[4,768]{1,0:T(4,128)S(1)}, f32[4,768]{1,0:T(4,128)}, u32[]{:S(2)}) copy-start(f32[4,768]{1,0:T(4,128)} %vec_ref.7) | copy-start | bytes 36868
  312.5 163.0 %copy-start.23 = (f32[4,768]{1,0:T(4,128)S(1)}, f32[4,768]{1,0:T(4,128)}, u32[]{:S(2)}) copy-start(f32[4,768]{1,0:T(4,128)} %param.63) | copy-start | bytes 36868
  312.6 163.0 %copy-start.24 = (f32[4,768]{1,0:T(4,128)S(1)}, f32[4,768]{1,0:T(4,128)}, u32[]{:S(2)}) copy-start(f32[4,768]{1,0:T(4,128)} %param.64) | copy-start | bytes 36868
  312.6 164.3 %copy-start = (f32[96,1000]{1,0:T(8,128)S(1)}, f32[96,1000]{1,0:T(8,128)}, u32[]{:S(2)}) copy-start(f32[96,1000]{1,0:T(8,128)} %param.59) | copy-start | bytes 1152004
  312.6 164.3 %copy-start.6 = (f32[96,1000]{1,0:T(8,128)S(1)}, f32[96,1000]{1,0:T(8,128)}, u32[]{:S(2)}) copy-start(f32[96,1000]{1,0:T(8,128)} %param.60) | copy-start | bytes 1152004
  312.6 164.3 %copy-start.7 = (f32[96,1000]{1,0:T(8,128)S(1)}, f32[96,1000]{1,0:T(8,128)}, u32[]{:S(2)}) copy-start(f32[96,1000]{1,0:T(8,128)} %param.61) | copy-start | bytes 1152004
  312.6 166.6 %copy-start.9 = (f32[96,768]{1,0:T(8,128)S(1)}, f32[96,768]{1,0:T(8,128)}, u32[]{:S(2)}) copy-start(f32[96,768]{1,0:T(8,128)} %param.54) | copy-start | bytes 884740
  312.6 166.6 %copy-start.10 = (f32[96,768]{1,0:T(8,128)S(1)}, f32[96,768]{1,0:T(8,128)}, u32[]{:S(2)}) copy-start(f32[96,768]{1,0:T(8,128)} %param.55) | copy-start | bytes 884740
  468.2 13.1 %copy-start.18 = (f32[192,96]{1,0:T(8,128)S(1)}, f32[192,96]{1,0:T(8,128)}, u32[]{:S(2)}) copy-start(f32[192,96]{1,0:T(8,128)} %param.51) | copy-start | bytes 221188
  468.2 13.2 %copy-start.19 = (f32[192,96]{1,0:T(8,128)S(1)}, f32[192,96]{1,0:T(8,128)}, u32[]{:S(2)}) copy-start(f32[192,96]{1,0:T(8,128)} %param.52) | copy-start | bytes 221188
  468.2 13.3 %copy-start.17 = (f32[96,192]{1,0:T(8,128)S(1)}, f32[96,192]{1,0:T(8,128)}, u32[]{:S(2)}) copy-start(f32[96,192]{1,0:T(8,128)} %get-tuple-element.147) | copy-start | bytes 221188
  476.9 6.9 %copy-start.15 = (f32[96,576]{1,0:T(8,128)S(1)}, f32[96,576]{1,0:T(8,128)}, u32[]{:S(2)}) copy-start(f32[96,576]{1,0:T(8,128)} %get-tuple-element.146) | copy-start | bytes 663556
  476.9 7.1 %copy-start.12 = (f32[96,3,192]{2,0,1:T(8,128)S(1)}, f32[96,3,192]{2,0,1:T(8,128)}, u32[]{:S(2)}) copy-start(f32[96,3,192]{2,0,1:T(8,128)} %param.48) | copy-start | bytes 663556
  479.2 5.0 %copy-start.13 = (f32[96,3,192]{2,0,1:T(8,128)S(1)}, f32[96,3,192]{2,0,1:T(8,128)}, u32[]{:S(2)}) copy-start(f32[96,3,192]{2,0,1:T(8,128)} %param.49) | copy-start | bytes 663556
  479.2 5.2 %copy-start.4 = (f32[96,3,192]{2,0,1:T(8,128)S(1)}, f32[96,3,192]{2,0,1:T(8,128)}, u32[]{:S(2)}) copy-start(f32[96,3,192]{2,0,1:T(8,128)} %param.47) | copy-start | bytes 663556
  483.9 3.6 copy-start.8
  483.9 3.7 copy-start.14
  483.9 3.7 copy-start.20
  483.9 3.7 copy-start.21
  484.1 4.2 copy-start.2
  484.1 4.2 copy-start.3
  484.1 4.2 copy-start.11
